TPU v7x, 1024 devices: a whole 4x4x32 slice. The times are simulated.
1024 devices in a mesh: row: 64 (over z, core), col: 16 (over x, y).
Axes of the slice: x: 4, y: 4, z: 32, core: 2. Of those that a mesh axis runs over, the one named last changes fastest.
Arguments:
- eigvecs: float32 [49152, 2048], P(('row', 'col')), may hold values from -6 to 6
- reflectors: float32 [3, 49152, 512], P(None, 'row'), may hold values from -0.15625 to 0.15625
- t_factor: float32 [3, 512, 512], replicated, as said below
- offsets: int32 [3], replicated, may hold values from 0 to 48640, as said below
Outputs:
- updated: float32 [49152, 2048], P('row', 'col')
Inputs may be any that keep to these rules, and one draw needn't show every extreme that they name: Each panel's vectors begin on consecutive rows offsets[p] to offsets[p] + 511; some panel starts at row 0 and some at row 48640. `t_factor`: each panel's factor is upper triangular with a diagonal between 0.25 and 2.
All inputs are finite; a program needn't handle non-finite values.
Results may differ from a plain program's by a relative error of at most 0.00014.
Values sent between devices are 32-bit elements; how exact they have to be, the bound alone decides.
A program may use at most 32 MiB of HBM per device.

v0:
```python
import jax
import jax.numpy as jnp
from jax import lax
from jax.sharding import PartitionSpec as P


def per_device(eigvecs, reflectors, t_factor, offsets):
    current = lax.all_to_all(eigvecs, "col", split_axis=1, concat_axis=0, tiled=True)
    rows_here = reflectors.shape[1]
    panel_width = reflectors.shape[2]
    first_row = lax.axis_index("row") * rows_here
    row_index = first_row + lax.broadcasted_iota(jnp.int32, (rows_here, 1), 0)
    column = lax.broadcasted_iota(jnp.int32, (1, panel_width), 1)
    for panel in range(reflectors.shape[0]):
        starts = offsets[panel] + column
        masked = jnp.where(
            row_index > starts,
            reflectors[panel],
            jnp.where(row_index == starts, jnp.float32(1.0), jnp.float32(0.0)),
        )
        partial_value = lax.dot_general(
            masked,
            current,
            (((0,), (0,)), ((), ())),
            precision=lax.Precision.HIGHEST,
            preferred_element_type=jnp.float32,
        )
        inner_sums = lax.psum(partial_value, "row")
        scaled = jnp.dot(
            t_factor[panel],
            inner_sums,
            precision=lax.Precision.HIGHEST,
            preferred_element_type=jnp.float32,
        )
        current = current - jnp.dot(
            masked, scaled, precision=lax.Precision.HIGHEST, preferred_element_type=jnp.float32
        )
    return current


def solution(mesh):
    return jax.shard_map(
        per_device,
        mesh=mesh,
        in_specs=(P(("row", "col"), None), P(None, "row", None), P(), P()),
        out_specs=P("row", "col"),
        check_vma=False,
    )
```

profile of v0, /device:TPU:1, one launch (start us, length us, event | category | flops | bytes accessed | tf_op | source)
XLA Modules:
  0.0 1206.9 jit_solution(16908154011662390414)
XLA Ops:
  6.5 1.0 copy-done
  7.5 0.8 copy_bitcast_fusion
  8.3 7.6 all-to-all-start
  15.9 0.0 all-reduce.4.cloned.1.call-start
  16.0 0.7 fusion.60
  16.6 0.6 iota_add_fusion.3
  17.3 6.6 all-to-all-done
  23.9 0.7 copy-done.2
  24.6 5.1 fusion
  29.7 0.0 all-reduce.4.cloned.1.call-update
  29.7 0.0 all-reduce.6.cloned.1.call-start
  29.8 0.7 iota_add_fusion.2
  30.5 391.6 %all-reduce.4.cloned.1.call-done = f32[512,128]{1,0:T(8,128)} async-done(((f32[512,128]{1,0:T(8,128)}), f32[512,128]{1,0:T(8,128)}) %all-reduce.4.cloned.1.call-update) | async-done | bytes 262160 | tf_op jit(solution)/shard_map/psum | solution.py:28
  422.0 2.2 fusion.19
  424.3 2.9 fusion.12
  427.2 0.0 copy-start.5
  427.2 0.7 copy-done.5
  428.0 4.9 fusion.13
  432.8 0.0 all-reduce.6.cloned.1.call-update
  432.9 0.2 all-reduce.8.cloned.1.call-start
  433.1 0.6 iota_add_fusion.1
  433.7 374.4 %all-reduce.6.cloned.1.call-done = f32[512,128]{1,0:T(8,128)} async-done(((f32[512,128]{1,0:T(8,128)}), f32[512,128]{1,0:T(8,128)}) %all-reduce.6.cloned.1.call-update) | async-done | bytes 262160 | tf_op jit(solution)/shard_map/psum | solution.py:28
  808.1 2.2 fusion.17
  810.3 0.0 copy-done.6
  810.4 2.9 convolution_subtract_fusion.1
  813.3 0.0 copy-start.7
  813.3 0.7 copy-done.7
  814.0 4.9 fusion.14
  818.9 0.0 all-reduce.8.cloned.1.call-update
  818.9 375.5 %all-reduce.8.cloned.1.call-done = f32[512,128]{1,0:T(8,128)} async-done(((f32[512,128]{1,0:T(8,128)}), f32[512,128]{1,0:T(8,128)}) %all-reduce.8.cloned.1.call-update) | async-done | bytes 262160 | tf_op jit(solution)/shard_map/psum | solution.py:28
  1194.4 2.2 fusion.15
  1196.7 3.7 convolution_subtract_fusion
  (12 shorter events, 0.0 us)
Async XLA Ops:
  6.5 1.0 copy-start
  6.5 9.4 copy-start.4
  8.3 15.6 %all-to-all-start = ((f32[48,16,128]{2,0,1:T(8,128)}), f32[48,16,128]{2,0,1:T(8,128)S(1)}, u32[]{:S(2)}, u32[]{:S(2)}) async-start(f32[48,16,128]{2,0,1:T(8,128)} %copy_bitcast_fusion), calls=%async_computation | async-start | bytes 786432 | tf_op jit(solution)/shard_map/all_to_all | solution.py:8
  15.9 406.1 %all-reduce.4.cloned.1.call-start = ((), (), s32[]{:S(2)}) async-start(), calls=%async_computation.1 | async-start | bytes 524288 | tf_op jit(solution)/shard_map/psum | solution.py:28
  23.9 0.7 copy-start.2
  24.6 397.4 %copy-start.1 = (f32[3,512,512]{2,1,0:T(8,128)S(1)}, f32[3,512,512]{2,1,0:T(8,128)}, u32[]{:S(2)}) copy-start(f32[3,512,512]{2,1,0:T(8,128)} %param.6) | copy-start | bytes 9437188
  29.7 778.4 %all-reduce.6.cloned.1.call-start = ((), (), s32[]{:S(2)}) async-start(), calls=%async_computation.2 | async-start | bytes 524288 | tf_op jit(solution)/shard_map/psum | solution.py:28
  422.0 2.3 copy-start.3
  427.2 0.7 copy-start.5
  432.9 761.6 %all-reduce.8.cloned.1.call-start = ((), (), s32[]{:S(2)}) async-start(), calls=%async_computation.3 | async-start | bytes 524288 | tf_op jit(solution)/shard_map/psum | solution.py:28
  808.1 2.3 copy-start.6
  813.3 0.7 copy-start.7
  1194.4 2.3 copy-start.8
Sparse Core Ops, SparseCore 0:
  29.8 392.1 all-reduce.3
  433.0 375.0 all-reduce.5
  819.0 375.3 all-reduce.7
where the time goes:
time: 1210 us
  waiting for transfers between devices  1150 us (95%)
  matrix products  31.1 us (3%)
  between operations  13.3 us (1%)
    psum x3, waiting for transfers between devices, per_device(): inner_sums = lax.psum(partial_value, 'row')  1140 us
  transfers between devices with their start and end apart: 4, of which 4 were waited for; matrix products, arithmetic and copies ran while one was open for 0% of the time, Pallas kernels for 0%

commit v1 on v0

v1 whole, which is shorter than its diff:
```python
import jax
import jax.numpy as jnp
from jax import lax
from jax.experimental import pallas as pl
from jax.experimental.pallas import tpu as pltpu
from jax.sharding import PartitionSpec as P

MESH = pl.DeviceIdType.MESH
F32 = jnp.float32
BF16 = jnp.bfloat16

NX, NY, NZ = 4, 4, 32
ROWS, PANEL, COLS = 768, 512, 128
PIECE = 48
TAIL = ROWS - PANEL
LAST = 64 * ROWS - PANEL
NEAR = (4, 3, -3, 2, -2, 1, -1)
FAR = (16, 8, -8)
XY = tuple((a, b) for a in range(NX) for b in range(NY) if (a, b) != (0, 0))
CHUNK = COLS // 8
GCHUNK = 8


def split(value):
    hi = value.astype(BF16)
    return hi, (value - hi.astype(F32)).astype(BF16)


def mm(a, b):
    return lax.dot_general(a, b, (((1,), (0,)), ((), ())), preferred_element_type=F32)


def mm_nt(a, b):
    return lax.dot_general(a, b, (((1,), (1,)), ((), ())), preferred_element_type=F32)


def mm_tn(a, b):
    return lax.dot_general(a, b, (((0,), (0,)), ((), ())), preferred_element_type=F32)


def three(dot, ah, al, bh, bl):
    return dot(ah, bh) + (dot(ah, bl) + dot(al, bh))


def kernel(
    off_ref, x_hbm, v_hbm, t_hbm, out_ref,
    cur, v3, t3, vh, vl, ch, cl, th, tl, ph, pl_, xs, w2, wpair, wsum, wrs, wx, wmine, wfull,
    gpart, gpair, gsum, grs, gx, gmine, gfull,
    load_sem, own_sem, a2a_s, a2a_r, gp_s, gp_r, wp_s, wp_r, grs_s, grs_r, wrs_s, wrs_r,
    gx_s, gx_r, wx_s, wx_r, gag_s, gag_r, wag_s, wag_r, gxy_s, gxy_r, gc_s, gc_r, wc_s, wc_r, far_sem,
):
    row, col = lax.axis_index("row"), lax.axis_index("col")
    z, core = row // 2, lax.rem(row, 2)
    x, y = col // NY, lax.rem(col, NY)
    other = 1 - core

    def along_z(d):
        return (lax.rem(z + (d + NZ), NZ) * 2 + core, col)

    def in_plane(a, b):
        return (row, lax.rem(x + a, NX) * NY + lax.rem(y + b, NY))

    partner = (z * 2 + other, col)

    def remote(src, dst, ssem, rsem, to):
        copy = pltpu.make_async_remote_copy(
            src_ref=src, dst_ref=dst, send_sem=ssem, recv_sem=rsem, device_id=to, device_id_type=MESH
        )
        copy.start()
        return copy

    barrier = pltpu.get_barrier_semaphore()
    greet = [in_plane(a, b) for a, b in XY] + [along_z(d) for d in (4, -4, 3, -3, 2, -2, 1, -1)] + [partner]
    for to in greet:
        pl.semaphore_signal(barrier, inc=1, device_id=to, device_id_type=MESH)

    loads = [pltpu.make_async_copy(v_hbm.at[p], v3.at[p], load_sem.at[p]) for p in range(3)]
    loads += [pltpu.make_async_copy(t_hbm, t3, load_sem.at[3])]
    for load in loads:
        load.start()
    mine = pl.ds(pl.multiple_of(col * PIECE, PIECE), PIECE)
    own = pltpu.make_async_copy(
        x_hbm.at[:, pl.ds(pl.multiple_of(col * COLS, COLS), COLS)], cur.at[mine, :], own_sem
    )
    own.start()

    pl.semaphore_wait(barrier, len(greet))
    a2a = []
    for n, (a, b) in enumerate(XY):
        to = in_plane(a, b)
        src = x_hbm.at[:, pl.ds(pl.multiple_of(to[1] * COLS, COLS), COLS)]
        a2a.append(remote(src, cur.at[mine, :], a2a_s.at[n], a2a_r.at[n], to))
    for d in (4, -4):
        pl.semaphore_signal(far_sem.at[0], inc=1, device_id=along_z(d), device_id_type=MESH)

    c = jnp.where(off_ref[0] == LAST, 0, jnp.where(off_ref[1] == LAST, 1, 2))
    pa = jnp.where(c == 0, 1, 0)
    pb = jnp.where(c == 2, 1, 2)
    off_a, off_b = off_ref[pa], off_ref[pb]

    def masked(panel, start, first, count):
        value = v3[panel, pl.ds(first, count), :]
        step = (
            row * ROWS + first - start
            + lax.broadcasted_iota(jnp.int32, (count, PANEL), 0)
            - lax.broadcasted_iota(jnp.int32, (count, PANEL), 1)
        )
        return jnp.where(step > 0, value, jnp.where(step == 0, F32(1.0), F32(0.0)))

    for load in loads:
        load.wait()

    R = 64

    def prepare(i, _):
        first = pl.multiple_of(i * R, R)
        hi, lo = split(masked(pa, off_a, first, R))
        vh[0, pl.ds(first, R), :] = hi
        vl[0, pl.ds(first, R), :] = lo
        hi, lo = split(masked(pb, off_b, first, R))
        vh[1, pl.ds(first, R), :] = hi
        vl[1, pl.ds(first, R), :] = lo
        vh[2, pl.ds(first, R), :] = hi
        vl[2, pl.ds(first, R), :] = lo
        return 0

    lax.fori_loop(0, ROWS // R, prepare, 0)

    def prepare_c(i, _):
        first = pl.multiple_of(i * R, R)
        hi, lo = split(masked(c, LAST, TAIL + first, R))
        ch[pl.ds(first, R), :] = hi
        cl[pl.ds(first, R), :] = lo
        for s, panel in ((0, pa), (1, pb), (2, c)):
            hi, lo = split(t3[panel, pl.ds(first, R), :])
            th[s, pl.ds(first, R), :] = hi
            tl[s, pl.ds(first, R), :] = lo
        return 0

    lax.fori_loop(0, PANEL // R, prepare_c, 0)

    M = 128

    def project(i, _):
        rows = pl.ds(pl.multiple_of(i * M, M), M)
        hi, lo = split(three(mm, ch[rows, :], cl[rows, :], th[2], tl[2]))
        hi, lo = split(three(mm_nt, hi, lo, ch[...], cl[...]))
        ph[rows, :] = hi
        pl_[rows, :] = lo
        return 0

    lax.fori_loop(0, PANEL // M, project, 0)

    def through(i, _):
        cols = pl.ds(pl.multiple_of(i * M, M), M)
        rows = pl.ds(pl.multiple_of(TAIL + i * M, M), M)
        tail = pl.ds(TAIL, PANEL)
        moved = three(mm_tn, ph[:, cols], pl_[:, cols], vh[2, tail, :], vl[2, tail, :])
        value = masked(pb, off_b, TAIL + i * M, M)
        hi, lo = split(jnp.where(c == 1, value - moved, value))
        vh[1, rows, :] = hi
        vl[1, rows, :] = lo
        return 0

    lax.fori_loop(0, PANEL // M, through, 0)

    gi, gj = x, y
    bi = pl.ds(pl.multiple_of(gi * 128, 128), 128)
    bj = pl.ds(pl.multiple_of(gj * 128, 128), 128)
    gpart[...] = three(mm_tn, vh[1, :, bi], vl[1, :, bi], vh[0, :, bj], vl[0, :, bj])
    gp = remote(gpart.at[pl.ds(pl.multiple_of(other * 64, 64), 64), :], gpair, gp_s, gp_r, partner)

    pl.semaphore_wait(far_sem.at[0], 2)
    for d in (8, -8):
        pl.semaphore_signal(far_sem.at[1], inc=1, device_id=along_z(d), device_id_type=MESH)

    gp.wait()
    gsum[...] = gpart[pl.ds(pl.multiple_of(core * 64, 64), 64), :] + gpair[...]
    slot = lax.rem(z, 8)

    def slot_of(d):
        return lax.rem(z + (d + NZ), 8)

    g_rs = []
    for n, d in enumerate(NEAR):
        src = gsum.at[pl.ds(pl.multiple_of(slot_of(d) * GCHUNK, GCHUNK), GCHUNK), :]
        g_rs.append(remote(src, grs.at[n], grs_s.at[n], grs_r.at[n], along_z(d)))

    own.wait()
    for copy in a2a:
        copy.wait()
    tail = pl.ds(TAIL, PANEL)
    xh, xl = split(cur[tail, :])
    moved = three(mm, ph[...], pl_[...], xh, xl)
    cur[tail, :] = jnp.where(c == 0, cur[tail, :] - moved, cur[tail, :])
    hi, lo = split(cur[...].T)
    xs[pl.ds(0, COLS), :] = hi
    xs[pl.ds(COLS, COLS), :] = lo

    def inner(p):
        both = mm(xs[...], vh[p])
        w2[p] = both[:COLS] + both[COLS:] + mm(xs[pl.ds(0, COLS), :], vl[p])

    inner(other)
    wp = remote(w2.at[other], wpair, wp_s, wp_r, partner)
    inner(core)
    wp.wait()
    wsum[...] = w2[core] + wpair[...]
    w_rs = []
    for n, d in enumerate(NEAR):
        src = wsum.at[pl.ds(pl.multiple_of(slot_of(d) * CHUNK, CHUNK), CHUNK), :]
        w_rs.append(remote(src, wrs.at[n], wrs_s.at[n], wrs_r.at[n], along_z(d)))

    for copy in g_rs:
        copy.wait()
    total = gsum[pl.ds(pl.multiple_of(slot * GCHUNK, GCHUNK), GCHUNK), :]
    for n in range(len(NEAR)):
        total = total + grs[n]
    gmine[...] = total
    pl.semaphore_wait(far_sem.at[1], 2)
    g_x = [remote(gmine, gx.at[n], gx_s.at[n], gx_r.at[n], along_z(d)) for n, d in enumerate(FAR)]

    for copy in w_rs:
        copy.wait()
    total = wsum[pl.ds(pl.multiple_of(slot * CHUNK, CHUNK), CHUNK), :]
    for n in range(len(NEAR)):
        total = total + wrs[n]
    wmine[...] = total
    w_x = [remote(wmine, wx.at[n], wx_s.at[n], wx_r.at[n], along_z(d)) for n, d in enumerate(FAR)]

    for copy in g_x:
        copy.wait()
    ghalf = gi * 128 + core * 64
    gspot = (pl.ds(pl.multiple_of(ghalf + slot * GCHUNK, GCHUNK), GCHUNK), bj)
    gfull[gspot] = (gmine[...] + gx[0]) + (gx[1] + gx[2])
    g_ag = [
        remote(gfull.at[gspot], gfull.at[gspot], gag_s.at[n], gag_r.at[n], along_z(d))
        for n, d in enumerate(NEAR)
    ]
    for copy in g_ag:
        copy.wait()
    gown = gfull.at[pl.ds(pl.multiple_of(ghalf, 64), 64), bj]
    g_xy = [remote(gown, gown, gxy_s.at[n], gxy_r.at[n], in_plane(a, b)) for n, (a, b) in enumerate(XY)]

    for copy in w_x:
        copy.wait()
    wspot = pl.ds(pl.multiple_of(slot * CHUNK, CHUNK), CHUNK)
    wfull[core, wspot, :] = (wmine[...] + wx[0]) + (wx[1] + wx[2])
    w_ag = [
        remote(wfull.at[core, wspot, :], wfull.at[core, wspot, :], wag_s.at[n], wag_r.at[n], along_z(d))
        for n, d in enumerate(NEAR)
    ]
    for copy in g_xy:
        copy.wait()
    g_c = []
    for i in range(4):
        part = gfull.at[pl.ds(pl.multiple_of(i * 128 + core * 64, 64), 64), :]
        g_c.append(remote(part, part, gc_s.at[i], gc_r.at[i], partner))
    for copy in w_ag:
        copy.wait()
    w_c = remote(wfull.at[core], wfull.at[core], wc_s, wc_r, partner)
    for copy in g_c:
        copy.wait()
    w_c.wait()

    hi, lo = split(wfull[0])
    sa = three(mm_nt, hi, lo, th[0], tl[0])
    sah, sal = split(sa)
    gh, gl = split(gfull[...])
    rest = wfull[1] - three(mm_nt, sah, sal, gh, gl)
    hi, lo = split(rest)
    sb = three(mm_nt, hi, lo, th[1], tl[1])
    sbh, sbl = split(sb)

    def update(p, value, sh, sl):
        both = mm_nt(vh[p], jnp.concatenate([sh, sl], axis=0))
        return value - (both[:, :COLS] + both[:, COLS:] + mm_nt(vl[p], sh))

    after_a = update(0, cur[...], sah, sal)
    cur[...] = after_a
    out_ref[...] = update(2, after_a, sbh, sbl)
    through_c = jnp.where(c == 1, cur[tail, :], out_ref[tail, :])
    xh, xl = split(through_c)
    moved = three(mm, ph[...], pl_[...], xh, xl)
    out_ref[tail, :] = jnp.where(c == 0, out_ref[tail, :], out_ref[tail, :] - moved)


def per_device(eigvecs, reflectors, t_factor, offsets):
    dma = pltpu.SemaphoreType.DMA
    near, far, plane = len(NEAR), len(FAR), len(XY)
    hbm, vmem = pl.BlockSpec(memory_space=pl.ANY), pltpu.VMEM
    return pl.pallas_call(
        kernel,
        out_shape=jax.ShapeDtypeStruct((ROWS, COLS), F32),
        in_specs=[pl.BlockSpec(memory_space=pltpu.SMEM), hbm, hbm, hbm],
        out_specs=pl.BlockSpec(memory_space=pltpu.VMEM),
        scratch_shapes=[
            vmem((ROWS, COLS), F32),
            vmem((3, ROWS, PANEL), F32),
            vmem((3, PANEL, PANEL), F32),
            vmem((3, ROWS, PANEL), BF16),
            vmem((3, ROWS, PANEL), BF16),
            vmem((PANEL, PANEL), BF16),
            vmem((PANEL, PANEL), BF16),
            vmem((3, PANEL, PANEL), BF16),
            vmem((3, PANEL, PANEL), BF16),
            vmem((PANEL, PANEL), BF16),
            vmem((PANEL, PANEL), BF16),
            vmem((2 * COLS, ROWS), BF16),
            vmem((2, COLS, PANEL), F32),
            vmem((COLS, PANEL), F32),
            vmem((COLS, PANEL), F32),
            vmem((near, CHUNK, PANEL), F32),
            vmem((far, CHUNK, PANEL), F32),
            vmem((CHUNK, PANEL), F32),
            vmem((2, COLS, PANEL), F32),
            vmem((128, 128), F32),
            vmem((64, 128), F32),
            vmem((64, 128), F32),
            vmem((near, GCHUNK, 128), F32),
            vmem((far, GCHUNK, 128), F32),
            vmem((GCHUNK, 128), F32),
            vmem((PANEL, PANEL), F32),
            dma((4,)), dma, dma((plane,)), dma((plane,)), dma, dma, dma, dma,
            dma((near,)), dma((near,)), dma((near,)), dma((near,)),
            dma((far,)), dma((far,)), dma((far,)), dma((far,)),
            dma((near,)), dma((near,)), dma((near,)), dma((near,)),
            dma((plane,)), dma((plane,)), dma((4,)), dma((4,)), dma, dma,
            pltpu.SemaphoreType.REGULAR((2,)),
        ],
        compiler_params=pltpu.CompilerParams(
            collective_id=0, has_side_effects=True, vmem_limit_bytes=48 * 2**20
        ),
        cost_estimate=pl.CostEstimate(flops=3 * 10**9, bytes_accessed=9 * 10**6, transcendentals=0),
        name="panels",
    )(offsets, eigvecs, reflectors, t_factor)


def solution(mesh):
    return jax.shard_map(
        per_device,
        mesh=mesh,
        in_specs=(P(("row", "col"), None), P(None, "row", None), P(), P()),
        out_specs=P("row", "col"),
        check_vma=False,
    )
```

time: 1210 us -> 86.8 us (0.07)
  waiting for transfers between devices: 1150 us -> 0 us
  Pallas kernels: 0 us -> 82.3 us
  matrix products: 31.1 us -> 0 us
  between operations: 13.3 us -> 0.01 us
    psum x3 -> x0, waiting for transfers between devices: 1140 us -> none  [per_device(): inner_sums = lax.psum(partial_value, 'row')]
    pallas_call x0 -> x1, Pallas kernels: none -> 82.3 us  [per_device(): pl.pallas_call(kernel, out_shape=jax.ShapeDtypeStruct((ROWS, COLS), F32),...]
    dot_general x9 -> x0, matrix products: 31.1 us -> none  [the longest x3 14.8 us: per_device(): lax.dot_general(masked, current, (((0,), (0,)), ((), ())), precision=lax....]
  transfers between devices with their start and end apart: 4 -> 0, of which waited for: 4 -> 0; matrix products, arithmetic and copies ran while one was open for 0% -> 0% of each run, Pallas kernels for 0% -> 0%
where the time goes in v1:
time: 86.8 us; the launch traced here: 86.6 us
  Pallas kernels  82.3 us (95%)
  local copies, waits for them, and re-layouts  4.29 us (5%)
    pallas_call x1, Pallas kernels, per_device(): pl.pallas_call(kernel, out_shape=jax.ShapeDtypeStruct((ROWS, COLS), F32),...  82.3 us
    unnamed x7, local copies, waits for them, and re-layouts  4.29 us

profile of v1, /device:TPU:1, one launch (start us, length us, event | category | flops | bytes accessed | tf_op | source)
XLA Modules:
  0.0 86.6 jit_solution(6993328090619234543)
XLA Ops:
  0.0 0.0 copy-start
  0.0 1.9 %copy-done = f32[3,512,512]{2,1,0:T(8,128)S(1)} copy-done((f32[3,512,512]{2,1,0:T(8,128)S(1)}, f32[3,512,512]{2,1,0:T(8,128)}, u32[]{:S(2)}) %copy-start) | copy-done | bytes 3145752
  1.9 0.0 copy-start.1
  1.9 1.0 %copy-done.1 = f32[48,2048]{1,0:T(8,128)S(1)} copy-done((f32[48,2048]{1,0:T(8,128)S(1)}, f32[48,2048]{1,0:T(8,128)}, u32[]{:S(2)}) %copy-start.1) | copy-done | bytes 393240
  2.9 0.0 copy-start.2
  2.9 0.7 copy-done.2
  3.5 82.3 %panels.1 = f32[768,128]{1,0:T(8,128)S(1)} custom-call(s32[3]{0:T(128)S(1)} %copy-done.2, f32[48,2048]{1,0:T(8,128)S(1)} %copy-done.1, f32[3,768,512]{2,1,0:T(8,128)} %v_hbm.1, f32[3,512,512]{2,1,0:T(8,128)S(1)} %copy-done), custom_call_target="tpu_custom_call" | custom-call | flops 3000000000 | bytes 9000000 | tf_op jit(solution)/shard_map/panels/pallas_call | solution.py:292
  85.8 0.7 copy.6
Async XLA Ops:
  0.0 1.9 %copy-start = (f32[3,512,512]{2,1,0:T(8,128)S(1)}, f32[3,512,512]{2,1,0:T(8,128)}, u32[]{:S(2)}) copy-start(f32[3,512,512]{2,1,0:T(8,128)} %t_hbm.1) | copy-start | bytes 9437188
  1.9 1.0 %copy-start.1 = (f32[48,2048]{1,0:T(8,128)S(1)}, f32[48,2048]{1,0:T(8,128)}, u32[]{:S(2)}) copy-start(f32[48,2048]{1,0:T(8,128)} %x_hbm.1) | copy-start | bytes 1179652
  2.9 0.7 copy-start.2

commit v2 on v1

v2 whole, which is shorter than its diff:
```python
import jax
import jax.numpy as jnp
from jax import lax
from jax.experimental import pallas as pl
from jax.experimental.pallas import tpu as pltpu
from jax.sharding import PartitionSpec as P

MESH = pl.DeviceIdType.MESH
F32 = jnp.float32
BF16 = jnp.bfloat16

NX, NY, NZ = 4, 4, 32
ROWS, PANEL, COLS = 768, 512, 128
PIECE = 48
TAIL = ROWS - PANEL
LAST = 64 * ROWS - PANEL
NEAR = (4, 3, -3, 2, -2, 1, -1)
FAR = (16, 8, -8)
XY = tuple((a, b) for a in range(NX) for b in range(NY) if (a, b) != (0, 0))
HALF = COLS // 2
CHUNK = HALF // 8
GCHUNK = 8


def split(value):
    hi = value.astype(BF16)
    return hi, (value - hi.astype(F32)).astype(BF16)


def mm(a, b):
    return lax.dot_general(a, b, (((1,), (0,)), ((), ())), preferred_element_type=F32)


def mm_nt(a, b):
    return lax.dot_general(a, b, (((1,), (1,)), ((), ())), preferred_element_type=F32)


def mm_tn(a, b):
    return lax.dot_general(a, b, (((0,), (0,)), ((), ())), preferred_element_type=F32)


def three(dot, ah, al, bh, bl):
    return dot(ah, bh) + (dot(ah, bl) + dot(al, bh))


def kernel(
    off_ref, x_hbm, v_hbm, t_hbm, out_ref,
    xv, cur, v3, t3, vh, vl, qh, ql, ch, cl, th, tl, ph, pl_, xs, w2, wpair, wsum, wrs, wx, wmine, wfull,
    gpart, gpair, gsum, grs, gx, gmine, gfull,
    load_sem, own_sem, a2a_s, a2a_r, gp_s, gp_r, wp_s, wp_r, grs_s, grs_r, wrs_s, wrs_r,
    gx_s, gx_r, wx_s, wx_r, gag_s, gag_r, wag_s, wag_r, gxy_s, gxy_r, gc_s, gc_r, wc_s, wc_r, far0, far1,
):
    row, col = lax.axis_index("row"), lax.axis_index("col")
    z, core = row // 2, lax.rem(row, 2)
    x, y = col // NY, lax.rem(col, NY)
    other = 1 - core

    def along_z(d):
        return (lax.rem(z + (d + NZ), NZ) * 2 + core, col)

    def in_plane(a, b):
        return (row, lax.rem(x + a, NX) * NY + lax.rem(y + b, NY))

    partner = (z * 2 + other, col)

    def remote(src, dst, ssem, rsem, to):
        copy = pltpu.make_async_remote_copy(
            src_ref=src, dst_ref=dst, send_sem=ssem, recv_sem=rsem, device_id=to, device_id_type=MESH
        )
        copy.start()
        return copy

    barrier = pltpu.get_barrier_semaphore()
    greet = [in_plane(a, b) for a, b in XY] + [along_z(d) for d in (4, -4, 3, -3, 2, -2, 1, -1)] + [partner]
    for to in greet:
        pl.semaphore_signal(barrier, inc=1, device_id=to, device_id_type=MESH)

    xload = pltpu.make_async_copy(x_hbm, xv, load_sem.at[0])
    xload.start()
    vloads = [pltpu.make_async_copy(v_hbm.at[p], v3.at[p], load_sem.at[1 + p]) for p in range(3)]
    tload = pltpu.make_async_copy(t_hbm, t3, load_sem.at[4])
    for load in vloads + [tload]:
        load.start()

    c = jnp.where(off_ref[0] == LAST, 0, jnp.where(off_ref[1] == LAST, 1, 2))
    pa = jnp.where(c == 0, 1, 0)
    pb = jnp.where(c == 2, 1, 2)
    off_a, off_b = off_ref[pa], off_ref[pb]

    def masked(panel, start, first, count):
        value = v3[panel, pl.ds(first, count), :]
        step = (
            row * ROWS + first - start
            + lax.broadcasted_iota(jnp.int32, (count, PANEL), 0)
            - lax.broadcasted_iota(jnp.int32, (count, PANEL), 1)
        )
        return jnp.where(step > 0, value, jnp.where(step == 0, F32(1.0), F32(0.0)))

    mine = pl.ds(pl.multiple_of(col * PIECE, PIECE), PIECE)
    xload.wait()
    own = pltpu.make_async_copy(
        xv.at[:, pl.ds(pl.multiple_of(col * COLS, COLS), COLS)], cur.at[mine, :], own_sem
    )
    own.start()
    for load in vloads:
        load.wait()

    R = 64

    def prepare_c(i, _):
        first = pl.multiple_of(i * R, R)
        hi, lo = split(masked(c, LAST, TAIL + first, R))
        ch[pl.ds(first, R), :] = hi
        cl[pl.ds(first, R), :] = lo
        return 0

    lax.fori_loop(0, PANEL // R, prepare_c, 0)

    def prepare(i, _):
        first = pl.multiple_of(i * R, R)
        rows = pl.ds(first, R)
        hi, lo = split(masked(pa, off_a, first, R))
        vh[0, rows, :] = hi
        vl[0, rows, :] = lo
        qh[rows, :] = hi
        ql[rows, :] = lo
        hi, lo = split(masked(pb, off_b, first, R))
        vh[1, rows, :] = hi
        vl[1, rows, :] = lo
        return 0

    lax.fori_loop(0, ROWS // R, prepare, 0)

    tload.wait()

    def prepare_t(i, _):
        rows = pl.ds(pl.multiple_of(i * R, R), R)
        for s, panel in ((0, pa), (1, pb), (2, c)):
            hi, lo = split(t3[panel, rows, :])
            th[s, rows, :] = hi
            tl[s, rows, :] = lo
        return 0

    pl.semaphore_wait(barrier, len(greet))
    a2a = []
    for n, (a, b) in enumerate(XY):
        to = in_plane(a, b)
        src = xv.at[:, pl.ds(pl.multiple_of(to[1] * COLS, COLS), COLS)]
        a2a.append(remote(src, cur.at[mine, :], a2a_s.at[n], a2a_r.at[n], to))
    for d in (4, -4):
        pl.semaphore_signal(far0, inc=1, device_id=along_z(d), device_id_type=MESH)

    lax.fori_loop(0, PANEL // R, prepare_t, 0)

    M = 128

    def project(i, _):
        rows = pl.ds(pl.multiple_of(i * M, M), M)
        hi, lo = split(three(mm, ch[rows, :], cl[rows, :], th[2], tl[2]))
        hi, lo = split(three(mm_nt, hi, lo, ch[...], cl[...]))
        ph[rows, :] = hi
        pl_[rows, :] = lo
        return 0

    lax.fori_loop(0, PANEL // M, project, 0)
    tail = pl.ds(TAIL, PANEL)

    def through(i, _):
        rows = pl.ds(pl.multiple_of(i * M, M), M)
        there = pl.ds(pl.multiple_of(TAIL + i * M, M), M)
        moved = three(mm, ph[rows, :], pl_[rows, :], vh[0, tail, :], vl[0, tail, :])
        value = masked(pa, off_a, TAIL + i * M, M)
        hi, lo = split(jnp.where(c == 1, value - moved, value))
        qh[there, :] = hi
        ql[there, :] = lo
        return 0

    lax.fori_loop(0, PANEL // M, through, 0)

    gi, gj = x, y
    bi = pl.ds(pl.multiple_of(gi * 128, 128), 128)
    bj = pl.ds(pl.multiple_of(gj * 128, 128), 128)
    gpart[...] = three(mm_tn, vh[1, :, bi], vl[1, :, bi], qh[:, bj], ql[:, bj])
    gp = remote(gpart.at[pl.ds(pl.multiple_of(other * 64, 64), 64), :], gpair, gp_s, gp_r, partner)

    pl.semaphore_wait(far0, 2)
    for d in (8, -8):
        pl.semaphore_signal(far1, inc=1, device_id=along_z(d), device_id_type=MESH)

    gp.wait()
    gsum[...] = gpart[pl.ds(pl.multiple_of(core * 64, 64), 64), :] + gpair[...]
    slot = lax.rem(z, 8)

    def slot_of(d):
        return lax.rem(z + (d + NZ), 8)

    g_rs = []
    for n, d in enumerate(NEAR):
        src = gsum.at[pl.ds(pl.multiple_of(slot_of(d) * GCHUNK, GCHUNK), GCHUNK), :]
        g_rs.append(remote(src, grs.at[n], grs_s.at[n], grs_r.at[n], along_z(d)))

    own.wait()
    for copy in a2a:
        copy.wait()
    plain = cur[tail, :]
    xh, xl = split(plain)
    moved = plain - three(mm, ph[...], pl_[...], xh, xl)
    for_a = jnp.where(c == 0, moved, plain)
    for_b = jnp.where(c <= 1, moved, plain)
    cur[tail, :] = for_a

    def put(p, cols, value):
        hi, lo = split(value)
        xs[p, pl.ds(0, COLS), cols] = hi
        xs[p, pl.ds(COLS, COLS), cols] = lo

    first = cur[pl.ds(0, TAIL), :].T
    for p, last in ((0, for_a), (1, for_b)):
        put(p, pl.ds(0, TAIL), first)
        put(p, tail, last.T)

    def inner(p):
        both = mm(xs[p], vh[p])
        w2[p] = both[:COLS] + both[COLS:] + mm(xs[p, pl.ds(0, COLS), :], vl[p])

    halves = (0, 1)

    def half(h):
        return pl.ds(h * HALF, HALF)

    def spot(h, s):
        return pl.ds(pl.multiple_of(h * HALF + s * CHUNK, CHUNK), CHUNK)

    inner(other)
    w_p = [remote(w2.at[other, half(h), :], wpair.at[half(h), :], wp_s.at[h], wp_r.at[h], partner) for h in halves]
    inner(core)
    w_rs = []
    for h in halves:
        w_p[h].wait()
        wsum[half(h), :] = w2[core, half(h), :] + wpair[half(h), :]
        w_rs.append([
            remote(wsum.at[spot(h, slot_of(d)), :], wrs.at[h, n], wrs_s.at[h, n], wrs_r.at[h, n], along_z(d))
            for n, d in enumerate(NEAR)
        ])

    for copy in g_rs:
        copy.wait()
    total = gsum[pl.ds(pl.multiple_of(slot * GCHUNK, GCHUNK), GCHUNK), :]
    for n in range(len(NEAR)):
        total = total + grs[n]
    gmine[...] = total
    pl.semaphore_wait(far1, 2)
    g_x = [remote(gmine, gx.at[n], gx_s.at[n], gx_r.at[n], along_z(d)) for n, d in enumerate(FAR)]

    w_x = []
    for h in halves:
        for copy in w_rs[h]:
            copy.wait()
        total = wsum[spot(h, slot), :]
        for n in range(len(NEAR)):
            total = total + wrs[h, n]
        wmine[h] = total
        w_x.append([
            remote(wmine.at[h], wx.at[h, n], wx_s.at[h, n], wx_r.at[h, n], along_z(d))
            for n, d in enumerate(FAR)
        ])

    for copy in g_x:
        copy.wait()
    ghalf = gi * 128 + core * 64
    gspot = (pl.ds(pl.multiple_of(ghalf + slot * GCHUNK, GCHUNK), GCHUNK), bj)
    gfull[gspot] = (gmine[...] + gx[0]) + (gx[1] + gx[2])
    g_ag = [
        remote(gfull.at[gspot], gfull.at[gspot], gag_s.at[n], gag_r.at[n], along_z(d))
        for n, d in enumerate(NEAR)
    ]
    for copy in g_ag:
        copy.wait()
    gown = gfull.at[pl.ds(pl.multiple_of(ghalf, 64), 64), bj]
    g_xy = [remote(gown, gown, gxy_s.at[n], gxy_r.at[n], in_plane(a, b)) for n, (a, b) in enumerate(XY)]

    w_ag = []
    for h in halves:
        for copy in w_x[h]:
            copy.wait()
        at = wfull.at[core, spot(h, slot), :]
        wfull[core, spot(h, slot), :] = (wmine[h] + wx[h, 0]) + (wx[h, 1] + wx[h, 2])
        w_ag.append([
            remote(at, at, wag_s.at[h, n], wag_r.at[h, n], along_z(d)) for n, d in enumerate(NEAR)
        ])
    w_c = []

    def hand_over(h):
        for copy in w_ag[h]:
            copy.wait()
        at = wfull.at[core, half(h), :]
        w_c.append(remote(at, at, wc_s.at[h], wc_r.at[h], partner))

    hand_over(0)
    for copy in g_xy:
        copy.wait()
    g_c = []
    for i in range(4):
        part = gfull.at[pl.ds(pl.multiple_of(i * 128 + core * 64, 64), 64), :]
        g_c.append(remote(part, part, gc_s.at[i], gc_r.at[i], partner))
    hand_over(1)
    for copy in w_c + g_c:
        copy.wait()

    hi, lo = split(wfull[0])
    sa = three(mm_nt, hi, lo, th[0], tl[0])
    sah, sal = split(sa)
    gh, gl = split(gfull[...])
    rest = wfull[1] - three(mm_nt, sah, sal, gh, gl)
    hi, lo = split(rest)
    sb = three(mm_nt, hi, lo, th[1], tl[1])
    sbh, sbl = split(sb)

    def update(p, value, sh, sl):
        both = mm_nt(vh[p], jnp.concatenate([sh, sl], axis=0))
        return value - (both[:, :COLS] + both[:, COLS:] + mm_nt(vl[p], sh))

    after_a = update(0, cur[...], sah, sal)
    cur[...] = after_a
    out_ref[...] = update(1, after_a, sbh, sbl)
    through_c = jnp.where(c == 1, cur[tail, :], out_ref[tail, :])
    xh, xl = split(through_c)
    moved = three(mm, ph[...], pl_[...], xh, xl)
    out_ref[tail, :] = jnp.where(c == 0, out_ref[tail, :], out_ref[tail, :] - moved)


def per_device(eigvecs, reflectors, t_factor, offsets):
    dma = pltpu.SemaphoreType.DMA
    near, far, plane = len(NEAR), len(FAR), len(XY)
    hbm, vmem = pl.BlockSpec(memory_space=pl.ANY), pltpu.VMEM
    return pl.pallas_call(
        kernel,
        out_shape=jax.ShapeDtypeStruct((ROWS, COLS), F32),
        in_specs=[pl.BlockSpec(memory_space=pltpu.SMEM), hbm, hbm, hbm],
        out_specs=pl.BlockSpec(memory_space=pltpu.VMEM),
        scratch_shapes=[
            vmem((PIECE, COLS * NX * NY), F32),
            vmem((ROWS, COLS), F32),
            vmem((3, ROWS, PANEL), F32),
            vmem((3, PANEL, PANEL), F32),
            vmem((2, ROWS, PANEL), BF16),
            vmem((2, ROWS, PANEL), BF16),
            vmem((ROWS, PANEL), BF16),
            vmem((ROWS, PANEL), BF16),
            vmem((PANEL, PANEL), BF16),
            vmem((PANEL, PANEL), BF16),
            vmem((3, PANEL, PANEL), BF16),
            vmem((3, PANEL, PANEL), BF16),
            vmem((PANEL, PANEL), BF16),
            vmem((PANEL, PANEL), BF16),
            vmem((2, 2 * COLS, ROWS), BF16),
            vmem((2, COLS, PANEL), F32),
            vmem((COLS, PANEL), F32),
            vmem((COLS, PANEL), F32),
            vmem((2, near, CHUNK, PANEL), F32),
            vmem((2, far, CHUNK, PANEL), F32),
            vmem((2, CHUNK, PANEL), F32),
            vmem((2, COLS, PANEL), F32),
            vmem((128, 128), F32),
            vmem((64, 128), F32),
            vmem((64, 128), F32),
            vmem((near, GCHUNK, 128), F32),
            vmem((far, GCHUNK, 128), F32),
            vmem((GCHUNK, 128), F32),
            vmem((PANEL, PANEL), F32),
            dma((5,)), dma, dma((plane,)), dma((plane,)), dma, dma, dma((2,)), dma((2,)),
            dma((near,)), dma((near,)), dma((2, near)), dma((2, near)),
            dma((far,)), dma((far,)), dma((2, far)), dma((2, far)),
            dma((near,)), dma((near,)), dma((2, near)), dma((2, near)),
            dma((plane,)), dma((plane,)), dma((4,)), dma((4,)), dma((2,)), dma((2,)),
            pltpu.SemaphoreType.REGULAR, pltpu.SemaphoreType.REGULAR,
        ],
        compiler_params=pltpu.CompilerParams(
            collective_id=0, has_side_effects=True, vmem_limit_bytes=60 * 2**20
        ),
        cost_estimate=pl.CostEstimate(flops=3 * 10**9, bytes_accessed=9 * 10**6, transcendentals=0),
        name="panels",
    )(offsets, eigvecs, reflectors, t_factor)


def solution(mesh):
    return jax.shard_map(
        per_device,
        mesh=mesh,
        in_specs=(P(("row", "col"), None), P(None, "row", None), P(), P()),
        out_specs=P("row", "col"),
        check_vma=False,
    )
```

time: 86.8 us -> 83.4 us (0.961)
  local copies, waits for them, and re-layouts: 4.29 us -> 1.77 us
    unnamed x7 -> x1, local copies, waits for them, and re-layouts: 4.29 us -> 1.77 us
where the time goes in v2:
time: 83.4 us; the launch traced here: 83.3 us
  Pallas kernels  81.5 us (98%)
  local copies, waits for them, and re-layouts  1.77 us (2%)
    pallas_call x1, Pallas kernels, per_device(): pl.pallas_call(kernel, out_shape=jax.ShapeDtypeStruct((ROWS, COLS), F32),...  81.5 us
    unnamed x1, local copies, waits for them, and re-layouts  1.77 us

profile of v2, /device:TPU:1, one launch (start us, length us, event | category | flops | bytes accessed | tf_op | source)
XLA Modules:
  0.0 83.3 jit_solution(10948860815596633975)
XLA Ops:
  0.0 81.5 %panels.1 = f32[768,128]{1,0:T(8,128)} custom-call(s32[3]{0:T(128)} %off_ref.1, f32[48,2048]{1,0:T(8,128)} %x_hbm.1, f32[3,768,512]{2,1,0:T(8,128)} %v_hbm.1, f32[3,512,512]{2,1,0:T(8,128)} %t_hbm.1), custom_call_target="tpu_custom_call" | custom-call | flops 3000000000 | bytes 9000000 | tf_op jit(solution)/shard_map/panels/pallas_call | solution.py:336
  81.5 1.8 %copy.6 = f32[768,128]{1,0:T(8,128)} copy(f32[768,128]{1,0:T(8,128)} %panels.1) | data formatting | bytes 786432

commit v3 on v2

--- a/solution.py
+++ b/solution.py
@@ -45,7 +45,7 @@
 
 def kernel(
     off_ref, x_hbm, v_hbm, t_hbm, out_ref,
-    xv, cur, v3, t3, vh, vl, qh, ql, ch, cl, th, tl, ph, pl_, xs, w2, wpair, wsum, wrs, wx, wmine, wfull,
+    xv, cur, v3, t3, vh, vl, ch, cl, th, tl, ph, pl_, xs, w2, wpair, wsum, wrs, wx, wmine, wfull,
     gpart, gpair, gsum, grs, gx, gmine, gfull,
     load_sem, own_sem, a2a_s, a2a_r, gp_s, gp_r, wp_s, wp_r, grs_s, grs_r, wrs_s, wrs_r,
     gx_s, gx_r, wx_s, wx_r, gag_s, gag_r, wag_s, wag_r, gxy_s, gxy_r, gc_s, gc_r, wc_s, wc_r, far0, far1,
@@ -107,40 +107,17 @@
 
     R = 64
 
-    def prepare_c(i, _):
-        first = pl.multiple_of(i * R, R)
-        hi, lo = split(masked(c, LAST, TAIL + first, R))
-        ch[pl.ds(first, R), :] = hi
-        cl[pl.ds(first, R), :] = lo
-        return 0
-
-    lax.fori_loop(0, PANEL // R, prepare_c, 0)
-
-    def prepare(i, _):
-        first = pl.multiple_of(i * R, R)
-        rows = pl.ds(first, R)
-        hi, lo = split(masked(pa, off_a, first, R))
-        vh[0, rows, :] = hi
-        vl[0, rows, :] = lo
-        qh[rows, :] = hi
-        ql[rows, :] = lo
-        hi, lo = split(masked(pb, off_b, first, R))
-        vh[1, rows, :] = hi
-        vl[1, rows, :] = lo
-        return 0
-
-    lax.fori_loop(0, ROWS // R, prepare, 0)
-
-    tload.wait()
-
-    def prepare_t(i, _):
-        rows = pl.ds(pl.multiple_of(i * R, R), R)
-        for s, panel in ((0, pa), (1, pb), (2, c)):
-            hi, lo = split(t3[panel, rows, :])
-            th[s, rows, :] = hi
-            tl[s, rows, :] = lo
-        return 0
-
+    def prepare(s, panel, start):
+        def some(i, _):
+            first = pl.multiple_of(i * R, R)
+            hi, lo = split(masked(panel, start, first, R))
+            vh[s, pl.ds(first, R), :] = hi
+            vl[s, pl.ds(first, R), :] = lo
+            return 0
+
+        lax.fori_loop(0, ROWS // R, some, 0)
+
+    prepare(0, pa, off_a)
     pl.semaphore_wait(barrier, len(greet))
     a2a = []
     for n, (a, b) in enumerate(XY):
@@ -150,37 +127,55 @@
     for d in (4, -4):
         pl.semaphore_signal(far0, inc=1, device_id=along_z(d), device_id_type=MESH)
 
-    lax.fori_loop(0, PANEL // R, prepare_t, 0)
-
+    prepare(1, pb, off_b)
+    tload.wait()
+    tail = pl.ds(TAIL, PANEL)
+    end = jnp.where(row == 2 * NZ - 1, 1, 0)
     M = 128
 
-    def project(i, _):
-        rows = pl.ds(pl.multiple_of(i * M, M), M)
-        hi, lo = split(three(mm, ch[rows, :], cl[rows, :], th[2], tl[2]))
-        hi, lo = split(three(mm_nt, hi, lo, ch[...], cl[...]))
-        ph[rows, :] = hi
-        pl_[rows, :] = lo
-        return 0
-
-    lax.fori_loop(0, PANEL // M, project, 0)
-    tail = pl.ds(TAIL, PANEL)
-
-    def through(i, _):
-        rows = pl.ds(pl.multiple_of(i * M, M), M)
-        there = pl.ds(pl.multiple_of(TAIL + i * M, M), M)
-        moved = three(mm, ph[rows, :], pl_[rows, :], vh[0, tail, :], vl[0, tail, :])
-        value = masked(pa, off_a, TAIL + i * M, M)
-        hi, lo = split(jnp.where(c == 1, value - moved, value))
-        qh[there, :] = hi
-        ql[there, :] = lo
-        return 0
-
-    lax.fori_loop(0, PANEL // M, through, 0)
+    @pl.when(row == 2 * NZ - 1)
+    def _():
+        def prepare_c(i, _):
+            first = pl.multiple_of(i * R, R)
+            rows = pl.ds(first, R)
+            hi, lo = split(masked(c, LAST, TAIL + first, R))
+            ch[rows, :] = hi
+            cl[rows, :] = lo
+            hi, lo = split(t3[c, rows, :])
+            th[2, rows, :] = hi
+            tl[2, rows, :] = lo
+            return 0
+
+        lax.fori_loop(0, PANEL // R, prepare_c, 0)
+
+        def project(i, _):
+            rows = pl.ds(pl.multiple_of(i * M, M), M)
+            hi, lo = split(three(mm, ch[rows, :], cl[rows, :], th[2], tl[2]))
+            hi, lo = split(three(mm_nt, hi, lo, ch[...], cl[...]))
+            ph[rows, :] = hi
+            pl_[rows, :] = lo
+            return 0
+
+        lax.fori_loop(0, PANEL // M, project, 0)
+        vh[2, pl.ds(0, TAIL), :] = vh[0, pl.ds(0, TAIL), :]
+        vl[2, pl.ds(0, TAIL), :] = vl[0, pl.ds(0, TAIL), :]
+
+        def through(i, _):
+            rows = pl.ds(pl.multiple_of(i * M, M), M)
+            there = pl.ds(pl.multiple_of(TAIL + i * M, M), M)
+            moved = three(mm, ph[rows, :], pl_[rows, :], vh[0, tail, :], vl[0, tail, :])
+            value = masked(pa, off_a, TAIL + i * M, M)
+            hi, lo = split(jnp.where(c == 1, value - moved, value))
+            vh[2, there, :] = hi
+            vl[2, there, :] = lo
+            return 0
+
+        lax.fori_loop(0, PANEL // M, through, 0)
 
     gi, gj = x, y
     bi = pl.ds(pl.multiple_of(gi * 128, 128), 128)
     bj = pl.ds(pl.multiple_of(gj * 128, 128), 128)
-    gpart[...] = three(mm_tn, vh[1, :, bi], vl[1, :, bi], qh[:, bj], ql[:, bj])
+    gpart[...] = three(mm_tn, vh[1, :, bi], vl[1, :, bi], vh[2 * end, :, bj], vl[2 * end, :, bj])
     gp = remote(gpart.at[pl.ds(pl.multiple_of(other * 64, 64), 64), :], gpair, gp_s, gp_r, partner)
 
     pl.semaphore_wait(far0, 2)
@@ -202,26 +197,26 @@
     own.wait()
     for copy in a2a:
         copy.wait()
-    plain = cur[tail, :]
-    xh, xl = split(plain)
-    moved = plain - three(mm, ph[...], pl_[...], xh, xl)
-    for_a = jnp.where(c == 0, moved, plain)
-    for_b = jnp.where(c <= 1, moved, plain)
-    cur[tail, :] = for_a
-
     def put(p, cols, value):
         hi, lo = split(value)
         xs[p, pl.ds(0, COLS), cols] = hi
         xs[p, pl.ds(COLS, COLS), cols] = lo
 
-    first = cur[pl.ds(0, TAIL), :].T
-    for p, last in ((0, for_a), (1, for_b)):
-        put(p, pl.ds(0, TAIL), first)
-        put(p, tail, last.T)
+    @pl.when(row == 2 * NZ - 1)
+    def _():
+        plain = cur[tail, :]
+        xh, xl = split(plain)
+        moved = plain - three(mm, ph[...], pl_[...], xh, xl)
+        cur[tail, :] = jnp.where(c == 0, moved, plain)
+        put(1, pl.ds(0, TAIL), cur[pl.ds(0, TAIL), :].T)
+        put(1, tail, jnp.where(c <= 1, moved, plain).T)
+
+    put(0, pl.ds(0, ROWS), cur[...].T)
 
     def inner(p):
-        both = mm(xs[p], vh[p])
-        w2[p] = both[:COLS] + both[COLS:] + mm(xs[p, pl.ds(0, COLS), :], vl[p])
+        value = xs.at[p * end]
+        both = mm(value[...], vh[p])
+        w2[p] = both[:COLS] + both[COLS:] + mm(value[pl.ds(0, COLS), :], vl[p])
 
     halves = (0, 1)
 
@@ -252,6 +247,15 @@
     pl.semaphore_wait(far1, 2)
     g_x = [remote(gmine, gx.at[n], gx_s.at[n], gx_r.at[n], along_z(d)) for n, d in enumerate(FAR)]
 
+    def prepare_t(i, _):
+        rows = pl.ds(pl.multiple_of(i * R, R), R)
+        for s, panel in ((0, pa), (1, pb)):
+            hi, lo = split(t3[panel, rows, :])
+            th[s, rows, :] = hi
+            tl[s, rows, :] = lo
+        return 0
+
+    lax.fori_loop(0, PANEL // R, prepare_t, 0)
     w_x = []
     for h in halves:
         for copy in w_rs[h]:
@@ -323,10 +327,13 @@
     after_a = update(0, cur[...], sah, sal)
     cur[...] = after_a
     out_ref[...] = update(1, after_a, sbh, sbl)
-    through_c = jnp.where(c == 1, cur[tail, :], out_ref[tail, :])
-    xh, xl = split(through_c)
-    moved = three(mm, ph[...], pl_[...], xh, xl)
-    out_ref[tail, :] = jnp.where(c == 0, out_ref[tail, :], out_ref[tail, :] - moved)
+
+    @pl.when(row == 2 * NZ - 1)
+    def _():
+        after_b = out_ref[tail, :]
+        xh, xl = split(jnp.where(c == 1, cur[tail, :], after_b))
+        moved = three(mm, ph[...], pl_[...], xh, xl)
+        out_ref[tail, :] = jnp.where(c == 0, after_b, after_b - moved)
 
 
 def per_device(eigvecs, reflectors, t_factor, offsets):
@@ -343,10 +350,8 @@
             vmem((ROWS, COLS), F32),
             vmem((3, ROWS, PANEL), F32),
             vmem((3, PANEL, PANEL), F32),
-            vmem((2, ROWS, PANEL), BF16),
-            vmem((2, ROWS, PANEL), BF16),
-            vmem((ROWS, PANEL), BF16),
-            vmem((ROWS, PANEL), BF16),
+            vmem((3, ROWS, PANEL), BF16),
+            vmem((3, ROWS, PANEL), BF16),
             vmem((PANEL, PANEL), BF16),
             vmem((PANEL, PANEL), BF16),
             vmem((3, PANEL, PANEL), BF16),
@@ -376,7 +381,7 @@
             pltpu.SemaphoreType.REGULAR, pltpu.SemaphoreType.REGULAR,
         ],
         compiler_params=pltpu.CompilerParams(
-            collective_id=0, has_side_effects=True, vmem_limit_bytes=60 * 2**20
+            collective_id=0, has_side_effects=True, vmem_limit_bytes=54600 * 2**10
         ),
         cost_estimate=pl.CostEstimate(flops=3 * 10**9, bytes_accessed=9 * 10**6, transcendentals=0),
         name="panels",

time: 83.4 us -> 78.9 us (0.946)
  Pallas kernels: 81.5 us -> 77.3 us
    pallas_call x1, Pallas kernels: 81.5 us -> 77.3 us  [per_device(): pl.pallas_call(kernel, out_shape=jax.ShapeDtypeStruct((ROWS, COLS), F32),...]
    unnamed x1 -> x3, local copies, waits for them, and re-layouts: 1.77 us -> 1.4 us
where the time goes in v3:
time: 78.9 us; the launch traced here: 78.8 us
  Pallas kernels  77.3 us (98%)
  local copies, waits for them, and re-layouts  1.4 us (2%)
    pallas_call x1, Pallas kernels, per_device(): pl.pallas_call(kernel, out_shape=jax.ShapeDtypeStruct((ROWS, COLS), F32),...  77.3 us

profile of v3, /device:TPU:1, one launch (start us, length us, event | category | flops | bytes accessed | tf_op | source)
XLA Modules:
  0.0 78.8 jit_solution(3526679911423110416)
XLA Ops:
  0.0 0.0 copy-start
  0.0 0.7 copy-done
  0.7 77.3 %panels.1 = f32[768,128]{1,0:T(8,128)S(1)} custom-call(s32[3]{0:T(128)S(1)} %copy-done, f32[48,2048]{1,0:T(8,128)} %x_hbm.1, f32[3,768,512]{2,1,0:T(8,128)} %v_hbm.1, f32[3,512,512]{2,1,0:T(8,128)} %t_hbm.1), custom_call_target="tpu_custom_call" | custom-call | flops 3000000000 | bytes 9000000 | tf_op jit(solution)/shard_map/panels/pallas_call | solution.py:343
  78.0 0.7 copy.6
Async XLA Ops:
  0.0 0.7 copy-start

commit v4 on v3

--- a/solution.py
+++ b/solution.py
@@ -15,7 +15,7 @@
 TAIL = ROWS - PANEL
 LAST = 64 * ROWS - PANEL
 NEAR = (4, 3, -3, 2, -2, 1, -1)
-FAR = (16, 8, -8)
+FAR = (12, -12, 4, -4)
 XY = tuple((a, b) for a in range(NX) for b in range(NY) if (a, b) != (0, 0))
 HALF = COLS // 2
 CHUNK = HALF // 8
@@ -45,7 +45,7 @@
 
 def kernel(
     off_ref, x_hbm, v_hbm, t_hbm, out_ref,
-    xv, cur, v3, t3, vh, vl, ch, cl, th, tl, ph, pl_, xs, w2, wpair, wsum, wrs, wx, wmine, wfull,
+    xv, cur, v3, t3, vh, vl, ch, cl, th, tl, ph, pl_, xs, sah, sal, w2, wpair, wsum, wrs, wx, wmine, wfull,
     gpart, gpair, gsum, grs, gx, gmine, gfull,
     load_sem, own_sem, a2a_s, a2a_r, gp_s, gp_r, wp_s, wp_r, grs_s, grs_r, wrs_s, wrs_r,
     gx_s, gx_r, wx_s, wx_r, gag_s, gag_r, wag_s, wag_r, gxy_s, gxy_r, gc_s, gc_r, wc_s, wc_r, far0, far1,
@@ -54,6 +54,7 @@
     z, core = row // 2, lax.rem(row, 2)
     x, y = col // NY, lax.rem(col, NY)
     other = 1 - core
+    part = 1 - core
 
     def along_z(d):
         return (lax.rem(z + (d + NZ), NZ) * 2 + core, col)
@@ -79,7 +80,7 @@
     xload.start()
     vloads = [pltpu.make_async_copy(v_hbm.at[p], v3.at[p], load_sem.at[1 + p]) for p in range(3)]
     tload = pltpu.make_async_copy(t_hbm, t3, load_sem.at[4])
-    for load in vloads + [tload]:
+    for load in vloads:
         load.start()
 
     c = jnp.where(off_ref[0] == LAST, 0, jnp.where(off_ref[1] == LAST, 1, 2))
@@ -102,22 +103,6 @@
         xv.at[:, pl.ds(pl.multiple_of(col * COLS, COLS), COLS)], cur.at[mine, :], own_sem
     )
     own.start()
-    for load in vloads:
-        load.wait()
-
-    R = 64
-
-    def prepare(s, panel, start):
-        def some(i, _):
-            first = pl.multiple_of(i * R, R)
-            hi, lo = split(masked(panel, start, first, R))
-            vh[s, pl.ds(first, R), :] = hi
-            vl[s, pl.ds(first, R), :] = lo
-            return 0
-
-        lax.fori_loop(0, ROWS // R, some, 0)
-
-    prepare(0, pa, off_a)
     pl.semaphore_wait(barrier, len(greet))
     a2a = []
     for n, (a, b) in enumerate(XY):
@@ -127,7 +112,26 @@
     for d in (4, -4):
         pl.semaphore_signal(far0, inc=1, device_id=along_z(d), device_id_type=MESH)
 
+    for load in vloads:
+        load.wait()
+    tload.start()
+    R = 64
+
+    def prepare(s, panel, start):
+        def some(i, _):
+            first = pl.multiple_of(i * R, R)
+            hi, lo = split(masked(panel, start, first, R))
+            vh[s, pl.ds(first, R), :] = hi
+            vl[s, pl.ds(first, R), :] = lo
+            return 0
+
+        lax.fori_loop(0, ROWS // R, some, 0)
+
+    prepare(0, pa, off_a)
     prepare(1, pb, off_b)
+    pl.semaphore_wait(far0, 2)
+    for d in (4, -4):
+        pl.semaphore_signal(far1, inc=1, device_id=along_z(d), device_id_type=MESH)
     tload.wait()
     tail = pl.ds(TAIL, PANEL)
     end = jnp.where(row == 2 * NZ - 1, 1, 0)
@@ -178,13 +182,10 @@
     gpart[...] = three(mm_tn, vh[1, :, bi], vl[1, :, bi], vh[2 * end, :, bj], vl[2 * end, :, bj])
     gp = remote(gpart.at[pl.ds(pl.multiple_of(other * 64, 64), 64), :], gpair, gp_s, gp_r, partner)
 
-    pl.semaphore_wait(far0, 2)
-    for d in (8, -8):
-        pl.semaphore_signal(far1, inc=1, device_id=along_z(d), device_id_type=MESH)
-
     gp.wait()
     gsum[...] = gpart[pl.ds(pl.multiple_of(core * 64, 64), 64), :] + gpair[...]
     slot = lax.rem(z, 8)
+    final = lax.rem(z + 4, 8)
 
     def slot_of(d):
         return lax.rem(z + (d + NZ), 8)
@@ -226,13 +227,13 @@
     def spot(h, s):
         return pl.ds(pl.multiple_of(h * HALF + s * CHUNK, CHUNK), CHUNK)
 
-    inner(other)
-    w_p = [remote(w2.at[other, half(h), :], wpair.at[half(h), :], wp_s.at[h], wp_r.at[h], partner) for h in halves]
     inner(core)
+    w_p = [remote(w2.at[core, half(h), :], wpair.at[half(h), :], wp_s.at[h], wp_r.at[h], partner) for h in halves]
+    inner(part)
     w_rs = []
     for h in halves:
         w_p[h].wait()
-        wsum[half(h), :] = w2[core, half(h), :] + wpair[half(h), :]
+        wsum[half(h), :] = w2[part, half(h), :] + wpair[half(h), :]
         w_rs.append([
             remote(wsum.at[spot(h, slot_of(d)), :], wrs.at[h, n], wrs_s.at[h, n], wrs_r.at[h, n], along_z(d))
             for n, d in enumerate(NEAR)
@@ -272,8 +273,8 @@
     for copy in g_x:
         copy.wait()
     ghalf = gi * 128 + core * 64
-    gspot = (pl.ds(pl.multiple_of(ghalf + slot * GCHUNK, GCHUNK), GCHUNK), bj)
-    gfull[gspot] = (gmine[...] + gx[0]) + (gx[1] + gx[2])
+    gspot = (pl.ds(pl.multiple_of(ghalf + final * GCHUNK, GCHUNK), GCHUNK), bj)
+    gfull[gspot] = (gx[0] + gx[1]) + (gx[2] + gx[3])
     g_ag = [
         remote(gfull.at[gspot], gfull.at[gspot], gag_s.at[n], gag_r.at[n], along_z(d))
         for n, d in enumerate(NEAR)
@@ -287,8 +288,8 @@
     for h in halves:
         for copy in w_x[h]:
             copy.wait()
-        at = wfull.at[core, spot(h, slot), :]
-        wfull[core, spot(h, slot), :] = (wmine[h] + wx[h, 0]) + (wx[h, 1] + wx[h, 2])
+        at = wfull.at[part, spot(h, final), :]
+        wfull[part, spot(h, final), :] = (wx[h, 0] + wx[h, 1]) + (wx[h, 2] + wx[h, 3])
         w_ag.append([
             remote(at, at, wag_s.at[h, n], wag_r.at[h, n], along_z(d)) for n, d in enumerate(NEAR)
         ])
@@ -297,7 +298,7 @@
     def hand_over(h):
         for copy in w_ag[h]:
             copy.wait()
-        at = wfull.at[core, half(h), :]
+        at = wfull.at[part, half(h), :]
         w_c.append(remote(at, at, wc_s.at[h], wc_r.at[h], partner))
 
     hand_over(0)
@@ -305,28 +306,37 @@
         copy.wait()
     g_c = []
     for i in range(4):
-        part = gfull.at[pl.ds(pl.multiple_of(i * 128 + core * 64, 64), 64), :]
-        g_c.append(remote(part, part, gc_s.at[i], gc_r.at[i], partner))
+        strip = gfull.at[pl.ds(pl.multiple_of(i * 128 + core * 64, 64), 64), :]
+        g_c.append(remote(strip, strip, gc_s.at[i], gc_r.at[i], partner))
     hand_over(1)
-    for copy in w_c + g_c:
-        copy.wait()
-
-    hi, lo = split(wfull[0])
-    sa = three(mm_nt, hi, lo, th[0], tl[0])
-    sah, sal = split(sa)
-    gh, gl = split(gfull[...])
-    rest = wfull[1] - three(mm_nt, sah, sal, gh, gl)
-    hi, lo = split(rest)
-    sb = three(mm_nt, hi, lo, th[1], tl[1])
-    sbh, sbl = split(sb)
-
     def update(p, value, sh, sl):
         both = mm_nt(vh[p], jnp.concatenate([sh, sl], axis=0))
         return value - (both[:, :COLS] + both[:, COLS:] + mm_nt(vl[p], sh))
 
-    after_a = update(0, cur[...], sah, sal)
-    cur[...] = after_a
-    out_ref[...] = update(1, after_a, sbh, sbl)
+    def apply_a():
+        hi, lo = split(wfull[0])
+        hi, lo = split(three(mm_nt, hi, lo, th[0], tl[0]))
+        sah[...] = hi
+        sal[...] = lo
+        cur[...] = update(0, cur[...], hi, lo)
+
+    @pl.when(core == 1)
+    def _():
+        apply_a()
+
+    for copy in w_c:
+        copy.wait()
+
+    @pl.when(core == 0)
+    def _():
+        apply_a()
+
+    for copy in g_c:
+        copy.wait()
+    gh, gl = split(gfull[...])
+    hi, lo = split(wfull[1] - three(mm_nt, sah[...], sal[...], gh, gl))
+    hi, lo = split(three(mm_nt, hi, lo, th[1], tl[1]))
+    out_ref[...] = update(1, cur[...], hi, lo)
 
     @pl.when(row == 2 * NZ - 1)
     def _():
@@ -359,6 +369,8 @@
             vmem((PANEL, PANEL), BF16),
             vmem((PANEL, PANEL), BF16),
             vmem((2, 2 * COLS, ROWS), BF16),
+            vmem((COLS, PANEL), BF16),
+            vmem((COLS, PANEL), BF16),
             vmem((2, COLS, PANEL), F32),
             vmem((COLS, PANEL), F32),
             vmem((COLS, PANEL), F32),

time: 78.9 us -> 74.2 us (0.940)
  Pallas kernels: 77.3 us -> 72.6 us
    pallas_call x1, Pallas kernels: 77.3 us -> 72.6 us  [per_device(): pl.pallas_call(kernel, out_shape=jax.ShapeDtypeStruct((ROWS, COLS), F32),...]
where the time goes in v4:
time: 74.2 us; the launch traced here: 74.1 us
  Pallas kernels  72.6 us (98%)
  local copies, waits for them, and re-layouts  1.4 us (2%)
    pallas_call x1, Pallas kernels, per_device(): pl.pallas_call(kernel, out_shape=jax.ShapeDtypeStruct((ROWS, COLS), F32),...  72.6 us

profile of v4, /device:TPU:1, one launch (start us, length us, event | category | flops | bytes accessed | tf_op | source)
XLA Modules:
  0.0 74.1 jit_solution(13046393703382608321)
XLA Ops:
  0.0 0.0 copy-start
  0.0 0.7 copy-done
  0.7 72.6 %panels.1 = f32[768,128]{1,0:T(8,128)S(1)} custom-call(s32[3]{0:T(128)S(1)} %copy-done, f32[48,2048]{1,0:T(8,128)} %x_hbm.1, f32[3,768,512]{2,1,0:T(8,128)} %v_hbm.1, f32[3,512,512]{2,1,0:T(8,128)} %t_hbm.1), custom_call_target="tpu_custom_call" | custom-call | flops 3000000000 | bytes 9000000 | tf_op jit(solution)/shard_map/panels/pallas_call | solution.py:353
  73.3 0.7 %copy.6 = f32[768,128]{1,0:T(8,128)} copy(f32[768,128]{1,0:T(8,128)S(1)} %panels.1) | data formatting | bytes 786432
Async XLA Ops:
  0.0 0.7 copy-start

commit v5 on v4

--- a/solution.py
+++ b/solution.py
@@ -187,13 +187,26 @@
     slot = lax.rem(z, 8)
     final = lax.rem(z + 4, 8)
 
+    def near(h):
+        sign = 1 - 2 * lax.rem(core + h, 2)
+        return [(n, d * sign) for n, d in enumerate(NEAR)]
+
     def slot_of(d):
         return lax.rem(z + (d + NZ), 8)
 
     g_rs = []
-    for n, d in enumerate(NEAR):
+    for n, d in near(0):
         src = gsum.at[pl.ds(pl.multiple_of(slot_of(d) * GCHUNK, GCHUNK), GCHUNK), :]
         g_rs.append(remote(src, grs.at[n], grs_s.at[n], grs_r.at[n], along_z(d)))
+
+    for copy in g_rs:
+        copy.wait()
+    total = gsum[pl.ds(pl.multiple_of(slot * GCHUNK, GCHUNK), GCHUNK), :]
+    for n in range(len(NEAR)):
+        total = total + grs[n]
+    gmine[...] = total
+    pl.semaphore_wait(far1, 2)
+    g_x = [remote(gmine, gx.at[n], gx_s.at[n], gx_r.at[n], along_z(d)) for n, d in enumerate(FAR)]
 
     own.wait()
     for copy in a2a:
@@ -236,17 +249,8 @@
         wsum[half(h), :] = w2[part, half(h), :] + wpair[half(h), :]
         w_rs.append([
             remote(wsum.at[spot(h, slot_of(d)), :], wrs.at[h, n], wrs_s.at[h, n], wrs_r.at[h, n], along_z(d))
-            for n, d in enumerate(NEAR)
+            for n, d in near(h)
         ])
-
-    for copy in g_rs:
-        copy.wait()
-    total = gsum[pl.ds(pl.multiple_of(slot * GCHUNK, GCHUNK), GCHUNK), :]
-    for n in range(len(NEAR)):
-        total = total + grs[n]
-    gmine[...] = total
-    pl.semaphore_wait(far1, 2)
-    g_x = [remote(gmine, gx.at[n], gx_s.at[n], gx_r.at[n], along_z(d)) for n, d in enumerate(FAR)]
 
     def prepare_t(i, _):
         rows = pl.ds(pl.multiple_of(i * R, R), R)
@@ -258,7 +262,8 @@
 
     lax.fori_loop(0, PANEL // R, prepare_t, 0)
     w_x = []
-    for h in halves:
+
+    def exchange(h):
         for copy in w_rs[h]:
             copy.wait()
         total = wsum[spot(h, slot), :]
@@ -270,15 +275,16 @@
             for n, d in enumerate(FAR)
         ])
 
+    exchange(0)
     for copy in g_x:
         copy.wait()
     ghalf = gi * 128 + core * 64
     gspot = (pl.ds(pl.multiple_of(ghalf + final * GCHUNK, GCHUNK), GCHUNK), bj)
     gfull[gspot] = (gx[0] + gx[1]) + (gx[2] + gx[3])
     g_ag = [
-        remote(gfull.at[gspot], gfull.at[gspot], gag_s.at[n], gag_r.at[n], along_z(d))
-        for n, d in enumerate(NEAR)
+        remote(gfull.at[gspot], gfull.at[gspot], gag_s.at[n], gag_r.at[n], along_z(d)) for n, d in near(1)
     ]
+    exchange(1)
     for copy in g_ag:
         copy.wait()
     gown = gfull.at[pl.ds(pl.multiple_of(ghalf, 64), 64), bj]
@@ -291,7 +297,7 @@
         at = wfull.at[part, spot(h, final), :]
         wfull[part, spot(h, final), :] = (wx[h, 0] + wx[h, 1]) + (wx[h, 2] + wx[h, 3])
         w_ag.append([
-            remote(at, at, wag_s.at[h, n], wag_r.at[h, n], along_z(d)) for n, d in enumerate(NEAR)
+            remote(at, at, wag_s.at[h, n], wag_r.at[h, n], along_z(d)) for n, d in near(h)
         ])
     w_c = []
 

time: 74.2 us -> 72.6 us (0.978)
  Pallas kernels: 72.6 us -> 70.9 us
    pallas_call x1, Pallas kernels: 72.6 us -> 70.9 us  [per_device(): pl.pallas_call(kernel, out_shape=jax.ShapeDtypeStruct((ROWS, COLS), F32),...]
where the time goes in v5:
time: 72.6 us; the launch traced here: 72.3 us
  Pallas kernels  70.9 us (98%)
  local copies, waits for them, and re-layouts  1.4 us (2%)
    pallas_call x1, Pallas kernels, per_device(): pl.pallas_call(kernel, out_shape=jax.ShapeDtypeStruct((ROWS, COLS), F32),...  70.9 us

profile of v5, /device:TPU:1, one launch (start us, length us, event | category | flops | bytes accessed | tf_op | source)
XLA Modules:
  0.0 72.3 jit_solution(10621266794565378693)
XLA Ops:
  0.0 0.0 copy-start
  0.0 0.7 copy-done
  0.7 70.9 %panels.1 = f32[768,128]{1,0:T(8,128)S(1)} custom-call(s32[3]{0:T(128)S(1)} %copy-done, f32[48,2048]{1,0:T(8,128)} %x_hbm.1, f32[3,768,512]{2,1,0:T(8,128)} %v_hbm.1, f32[3,512,512]{2,1,0:T(8,128)} %t_hbm.1), custom_call_target="tpu_custom_call" | custom-call | flops 3000000000 | bytes 9000000 | tf_op jit(solution)/shard_map/panels/pallas_call | solution.py:359
  71.5 0.7 %copy.6 = f32[768,128]{1,0:T(8,128)} copy(f32[768,128]{1,0:T(8,128)S(1)} %panels.1) | data formatting | bytes 786432
Async XLA Ops:
  0.0 0.7 copy-start

commit v6 on v5

--- a/solution.py
+++ b/solution.py
@@ -17,7 +17,8 @@
 NEAR = (4, 3, -3, 2, -2, 1, -1)
 FAR = (12, -12, 4, -4)
 XY = tuple((a, b) for a in range(NX) for b in range(NY) if (a, b) != (0, 0))
-HALF = COLS // 2
+HALF, LANES = COLS // 2, 512
+PARTS = 2 * PANEL // LANES
 CHUNK = HALF // 8
 GCHUNK = 8
 
@@ -89,7 +90,13 @@
     off_a, off_b = off_ref[pa], off_ref[pb]
 
     def masked(panel, start, first, count):
-        value = v3[panel, pl.ds(first, count), :]
+        rows = pl.ds(first, count)
+        if panel is pa:
+            value = jnp.where(pa == 1, v3[1, rows, :], v3[0, rows, :])
+        elif panel is pb:
+            value = jnp.where(pb == 1, v3[1, rows, :], v3[2, rows, :])
+        else:
+            value = v3[panel, rows, :]
         step = (
             row * ROWS + first - start
             + lax.broadcasted_iota(jnp.int32, (count, PANEL), 0)
@@ -103,6 +110,21 @@
         xv.at[:, pl.ds(pl.multiple_of(col * COLS, COLS), COLS)], cur.at[mine, :], own_sem
     )
     own.start()
+    R = 64
+
+    def prepare(s, panel, start):
+        def some(i, _):
+            first = pl.multiple_of(i * R, R)
+            hi, lo = split(masked(panel, start, first, R))
+            vh[s, pl.ds(first, R), :] = hi
+            vl[s, pl.ds(first, R), :] = lo
+            return 0
+
+        lax.fori_loop(0, ROWS // R, some, 0)
+
+    vloads[0].wait()
+    vloads[1].wait()
+    prepare(0, pa, off_a)
     pl.semaphore_wait(barrier, len(greet))
     a2a = []
     for n, (a, b) in enumerate(XY):
@@ -112,30 +134,14 @@
     for d in (4, -4):
         pl.semaphore_signal(far0, inc=1, device_id=along_z(d), device_id_type=MESH)
 
-    for load in vloads:
-        load.wait()
+    vloads[2].wait()
     tload.start()
-    R = 64
-
-    def prepare(s, panel, start):
-        def some(i, _):
-            first = pl.multiple_of(i * R, R)
-            hi, lo = split(masked(panel, start, first, R))
-            vh[s, pl.ds(first, R), :] = hi
-            vl[s, pl.ds(first, R), :] = lo
-            return 0
-
-        lax.fori_loop(0, ROWS // R, some, 0)
-
-    prepare(0, pa, off_a)
     prepare(1, pb, off_b)
-    pl.semaphore_wait(far0, 2)
-    for d in (4, -4):
-        pl.semaphore_signal(far1, inc=1, device_id=along_z(d), device_id_type=MESH)
-    tload.wait()
     tail = pl.ds(TAIL, PANEL)
     end = jnp.where(row == 2 * NZ - 1, 1, 0)
     M = 128
+
+    tload.wait()
 
     @pl.when(row == 2 * NZ - 1)
     def _():
@@ -199,14 +205,9 @@
         src = gsum.at[pl.ds(pl.multiple_of(slot_of(d) * GCHUNK, GCHUNK), GCHUNK), :]
         g_rs.append(remote(src, grs.at[n], grs_s.at[n], grs_r.at[n], along_z(d)))
 
-    for copy in g_rs:
-        copy.wait()
-    total = gsum[pl.ds(pl.multiple_of(slot * GCHUNK, GCHUNK), GCHUNK), :]
-    for n in range(len(NEAR)):
-        total = total + grs[n]
-    gmine[...] = total
-    pl.semaphore_wait(far1, 2)
-    g_x = [remote(gmine, gx.at[n], gx_s.at[n], gx_r.at[n], along_z(d)) for n, d in enumerate(FAR)]
+    pl.semaphore_wait(far0, 2)
+    for d in (4, -4):
+        pl.semaphore_signal(far1, inc=1, device_id=along_z(d), device_id_type=MESH)
 
     own.wait()
     for copy in a2a:
@@ -232,23 +233,35 @@
         both = mm(value[...], vh[p])
         w2[p] = both[:COLS] + both[COLS:] + mm(value[pl.ds(0, COLS), :], vl[p])
 
-    halves = (0, 1)
+    halves = tuple(range(PARTS))
+
+    def lanes(h):
+        return pl.ds(h // 2 * LANES, LANES)
 
     def half(h):
-        return pl.ds(h * HALF, HALF)
+        return pl.ds(h % 2 * HALF, HALF), lanes(h)
 
     def spot(h, s):
-        return pl.ds(pl.multiple_of(h * HALF + s * CHUNK, CHUNK), CHUNK)
+        return pl.ds(pl.multiple_of(h % 2 * HALF + s * CHUNK, CHUNK), CHUNK), lanes(h)
 
     inner(core)
-    w_p = [remote(w2.at[core, half(h), :], wpair.at[half(h), :], wp_s.at[h], wp_r.at[h], partner) for h in halves]
+    w_p = [remote(w2.at[(core, *half(h))], wpair.at[half(h)], wp_s.at[h], wp_r.at[h], partner) for h in halves]
     inner(part)
+    for copy in g_rs:
+        copy.wait()
+    total = gsum[pl.ds(pl.multiple_of(slot * GCHUNK, GCHUNK), GCHUNK), :]
+    for n in range(len(NEAR)):
+        total = total + grs[n]
+    gmine[...] = total
+    pl.semaphore_wait(far1, 2)
+    g_x = [remote(gmine, gx.at[n], gx_s.at[n], gx_r.at[n], along_z(d)) for n, d in enumerate(FAR)]
+
     w_rs = []
     for h in halves:
         w_p[h].wait()
-        wsum[half(h), :] = w2[part, half(h), :] + wpair[half(h), :]
+        wsum[half(h)] = w2[(part, *half(h))] + wpair[half(h)]
         w_rs.append([
-            remote(wsum.at[spot(h, slot_of(d)), :], wrs.at[h, n], wrs_s.at[h, n], wrs_r.at[h, n], along_z(d))
+            remote(wsum.at[spot(h, slot_of(d))], wrs.at[h, n], wrs_s.at[h, n], wrs_r.at[h, n], along_z(d))
             for n, d in near(h)
         ])
 
@@ -266,7 +279,7 @@
     def exchange(h):
         for copy in w_rs[h]:
             copy.wait()
-        total = wsum[spot(h, slot), :]
+        total = wsum[spot(h, slot)]
         for n in range(len(NEAR)):
             total = total + wrs[h, n]
         wmine[h] = total
@@ -275,7 +288,8 @@
             for n, d in enumerate(FAR)
         ])
 
-    exchange(0)
+    for h in halves[: PARTS // 2]:
+        exchange(h)
     for copy in g_x:
         copy.wait()
     ghalf = gi * 128 + core * 64
@@ -284,7 +298,8 @@
     g_ag = [
         remote(gfull.at[gspot], gfull.at[gspot], gag_s.at[n], gag_r.at[n], along_z(d)) for n, d in near(1)
     ]
-    exchange(1)
+    for h in halves[PARTS // 2 :]:
+        exchange(h)
     for copy in g_ag:
         copy.wait()
     gown = gfull.at[pl.ds(pl.multiple_of(ghalf, 64), 64), bj]
@@ -294,8 +309,8 @@
     for h in halves:
         for copy in w_x[h]:
             copy.wait()
-        at = wfull.at[part, spot(h, final), :]
-        wfull[part, spot(h, final), :] = (wx[h, 0] + wx[h, 1]) + (wx[h, 2] + wx[h, 3])
+        at = wfull.at[(part, *spot(h, final))]
+        wfull[(part, *spot(h, final))] = (wx[h, 0] + wx[h, 1]) + (wx[h, 2] + wx[h, 3])
         w_ag.append([
             remote(at, at, wag_s.at[h, n], wag_r.at[h, n], along_z(d)) for n, d in near(h)
         ])
@@ -304,17 +319,18 @@
     def hand_over(h):
         for copy in w_ag[h]:
             copy.wait()
-        at = wfull.at[part, half(h), :]
+        at = wfull.at[(part, *half(h))]
         w_c.append(remote(at, at, wc_s.at[h], wc_r.at[h], partner))
 
-    hand_over(0)
+    for h in halves[:-1]:
+        hand_over(h)
     for copy in g_xy:
         copy.wait()
     g_c = []
     for i in range(4):
         strip = gfull.at[pl.ds(pl.multiple_of(i * 128 + core * 64, 64), 64), :]
         g_c.append(remote(strip, strip, gc_s.at[i], gc_r.at[i], partner))
-    hand_over(1)
+    hand_over(halves[-1])
     def update(p, value, sh, sl):
         both = mm_nt(vh[p], jnp.concatenate([sh, sl], axis=0))
         return value - (both[:, :COLS] + both[:, COLS:] + mm_nt(vl[p], sh))
@@ -380,9 +396,9 @@
             vmem((2, COLS, PANEL), F32),
             vmem((COLS, PANEL), F32),
             vmem((COLS, PANEL), F32),
-            vmem((2, near, CHUNK, PANEL), F32),
-            vmem((2, far, CHUNK, PANEL), F32),
-            vmem((2, CHUNK, PANEL), F32),
+            vmem((PARTS, near, CHUNK, LANES), F32),
+            vmem((PARTS, far, CHUNK, LANES), F32),
+            vmem((PARTS, CHUNK, LANES), F32),
             vmem((2, COLS, PANEL), F32),
             vmem((128, 128), F32),
             vmem((64, 128), F32),
@@ -391,11 +407,11 @@
             vmem((far, GCHUNK, 128), F32),
             vmem((GCHUNK, 128), F32),
             vmem((PANEL, PANEL), F32),
-            dma((5,)), dma, dma((plane,)), dma((plane,)), dma, dma, dma((2,)), dma((2,)),
-            dma((near,)), dma((near,)), dma((2, near)), dma((2, near)),
-            dma((far,)), dma((far,)), dma((2, far)), dma((2, far)),
-            dma((near,)), dma((near,)), dma((2, near)), dma((2, near)),
-            dma((plane,)), dma((plane,)), dma((4,)), dma((4,)), dma((2,)), dma((2,)),
+            dma((5,)), dma, dma((plane,)), dma((plane,)), dma, dma, dma((PARTS,)), dma((PARTS,)),
+            dma((near,)), dma((near,)), dma((PARTS, near)), dma((PARTS, near)),
+            dma((far,)), dma((far,)), dma((PARTS, far)), dma((PARTS, far)),
+            dma((near,)), dma((near,)), dma((PARTS, near)), dma((PARTS, near)),
+            dma((plane,)), dma((plane,)), dma((4,)), dma((4,)), dma((PARTS,)), dma((PARTS,)),
             pltpu.SemaphoreType.REGULAR, pltpu.SemaphoreType.REGULAR,
         ],
         compiler_params=pltpu.CompilerParams(

time: 72.6 us -> 71.2 us (0.981)
  Pallas kernels: 70.9 us -> 69.6 us
    pallas_call x1, Pallas kernels: 70.9 us -> 69.6 us  [per_device(): pl.pallas_call(kernel, out_shape=jax.ShapeDtypeStruct((ROWS, COLS), F32),...]
where the time goes in v6:
time: 71.2 us; the launch traced here: 71 us
  Pallas kernels  69.6 us (98%)
  local copies, waits for them, and re-layouts  1.4 us (2%)
    pallas_call x1, Pallas kernels, per_device(): pl.pallas_call(kernel, out_shape=jax.ShapeDtypeStruct((ROWS, COLS), F32),...  69.6 us

profile of v6, /device:TPU:1, one launch (start us, length us, event | category | flops | bytes accessed | tf_op | source)
XLA Modules:
  0.0 71.0 jit_solution(752692062663158355)
XLA Ops:
  0.0 0.0 copy-start
  0.0 0.7 copy-done
  0.7 69.6 %panels.1 = f32[768,128]{1,0:T(8,128)S(1)} custom-call(s32[3]{0:T(128)S(1)} %copy-done, f32[48,2048]{1,0:T(8,128)} %x_hbm.1, f32[3,768,512]{2,1,0:T(8,128)} %v_hbm.1, f32[3,512,512]{2,1,0:T(8,128)} %t_hbm.1), custom_call_target="tpu_custom_call" | custom-call | flops 3000000000 | bytes 9000000 | tf_op jit(solution)/shard_map/panels/pallas_call | solution.py:375
  70.2 0.7 %copy.6 = f32[768,128]{1,0:T(8,128)} copy(f32[768,128]{1,0:T(8,128)S(1)} %panels.1) | data formatting | bytes 786432
Async XLA Ops:
  0.0 0.7 copy-start

commit v7 on v6

--- a/solution.py
+++ b/solution.py
@@ -17,7 +17,7 @@
 NEAR = (4, 3, -3, 2, -2, 1, -1)
 FAR = (12, -12, 4, -4)
 XY = tuple((a, b) for a in range(NX) for b in range(NY) if (a, b) != (0, 0))
-HALF, LANES = COLS // 2, 512
+HALF, LANES = COLS // 2, 256
 PARTS = 2 * PANEL // LANES
 CHUNK = HALF // 8
 GCHUNK = 8
@@ -46,7 +46,7 @@
 
 def kernel(
     off_ref, x_hbm, v_hbm, t_hbm, out_ref,
-    xv, cur, v3, t3, vh, vl, ch, cl, th, tl, ph, pl_, xs, sah, sal, w2, wpair, wsum, wrs, wx, wmine, wfull,
+    xv, cur, v3, t3, vh, vl, ch, cl, th, tl, ph, pl_, xs, gh, gl, sag, w2, wpair, wsum, wrs, wx, wmine, wfull,
     gpart, gpair, gsum, grs, gx, gmine, gfull,
     load_sem, own_sem, a2a_s, a2a_r, gp_s, gp_r, wp_s, wp_r, grs_s, grs_r, wrs_s, wrs_r,
     gx_s, gx_r, wx_s, wx_r, gag_s, gag_r, wag_s, wag_r, gxy_s, gxy_r, gc_s, gc_r, wc_s, wc_r, far0, far1,
@@ -338,9 +338,12 @@
     def apply_a():
         hi, lo = split(wfull[0])
         hi, lo = split(three(mm_nt, hi, lo, th[0], tl[0]))
-        sah[...] = hi
-        sal[...] = lo
+        sag[...] = three(mm_nt, hi, lo, gh[...], gl[...])
         cur[...] = update(0, cur[...], hi, lo)
+
+    for copy in g_c:
+        copy.wait()
+    gh[...], gl[...] = split(gfull[...])
 
     @pl.when(core == 1)
     def _():
@@ -353,10 +356,7 @@
     def _():
         apply_a()
 
-    for copy in g_c:
-        copy.wait()
-    gh, gl = split(gfull[...])
-    hi, lo = split(wfull[1] - three(mm_nt, sah[...], sal[...], gh, gl))
+    hi, lo = split(wfull[1] - sag[...])
     hi, lo = split(three(mm_nt, hi, lo, th[1], tl[1]))
     out_ref[...] = update(1, cur[...], hi, lo)
 
@@ -391,8 +391,9 @@
             vmem((PANEL, PANEL), BF16),
             vmem((PANEL, PANEL), BF16),
             vmem((2, 2 * COLS, ROWS), BF16),
-            vmem((COLS, PANEL), BF16),
-            vmem((COLS, PANEL), BF16),
+            vmem((PANEL, PANEL), BF16),
+            vmem((PANEL, PANEL), BF16),
+            vmem((COLS, PANEL), F32),
             vmem((2, COLS, PANEL), F32),
             vmem((COLS, PANEL), F32),
             vmem((COLS, PANEL), F32),

time: 71.2 us -> 72.3 us (1.015)
  Pallas kernels: 69.6 us -> 70.7 us
    pallas_call x1, Pallas kernels: 69.6 us -> 70.7 us  [per_device(): pl.pallas_call(kernel, out_shape=jax.ShapeDtypeStruct((ROWS, COLS), F32),...]
where the time goes in v7:
time: 72.3 us; the launch traced here: 72.1 us
  Pallas kernels  70.7 us (98%)
  local copies, waits for them, and re-layouts  1.4 us (2%)
    pallas_call x1, Pallas kernels, per_device(): pl.pallas_call(kernel, out_shape=jax.ShapeDtypeStruct((ROWS, COLS), F32),...  70.7 us

profile of v7, /device:TPU:1, one launch (start us, length us, event | category | flops | bytes accessed | tf_op | source)
XLA Modules:
  0.0 72.1 jit_solution(780859561840362058)
XLA Ops:
  0.0 0.0 copy-start
  0.0 0.7 copy-done
  0.7 70.7 %panels.1 = f32[768,128]{1,0:T(8,128)S(1)} custom-call(s32[3]{0:T(128)S(1)} %copy-done, f32[48,2048]{1,0:T(8,128)} %x_hbm.1, f32[3,768,512]{2,1,0:T(8,128)} %v_hbm.1, f32[3,512,512]{2,1,0:T(8,128)} %t_hbm.1), custom_call_target="tpu_custom_call" | custom-call | flops 3000000000 | bytes 9000000 | tf_op jit(solution)/shard_map/panels/pallas_call | solution.py:375
  71.4 0.7 %copy.6 = f32[768,128]{1,0:T(8,128)} copy(f32[768,128]{1,0:T(8,128)S(1)} %panels.1) | data formatting | bytes 786432
Async XLA Ops:
  0.0 0.7 copy-start

commit v8 on v7

--- a/solution.py
+++ b/solution.py
@@ -17,7 +17,7 @@
 NEAR = (4, 3, -3, 2, -2, 1, -1)
 FAR = (12, -12, 4, -4)
 XY = tuple((a, b) for a in range(NX) for b in range(NY) if (a, b) != (0, 0))
-HALF, LANES = COLS // 2, 256
+HALF, LANES = COLS // 2, 512
 PARTS = 2 * PANEL // LANES
 CHUNK = HALF // 8
 GCHUNK = 8
@@ -65,11 +65,14 @@
 
     partner = (z * 2 + other, col)
 
+    sent = []
+
     def remote(src, dst, ssem, rsem, to):
         copy = pltpu.make_async_remote_copy(
             src_ref=src, dst_ref=dst, send_sem=ssem, recv_sem=rsem, device_id=to, device_id_type=MESH
         )
         copy.start()
+        sent.append(copy)
         return copy
 
     barrier = pltpu.get_barrier_semaphore()
@@ -188,7 +191,7 @@
     gpart[...] = three(mm_tn, vh[1, :, bi], vl[1, :, bi], vh[2 * end, :, bj], vl[2 * end, :, bj])
     gp = remote(gpart.at[pl.ds(pl.multiple_of(other * 64, 64), 64), :], gpair, gp_s, gp_r, partner)
 
-    gp.wait()
+    gp.wait_recv()
     gsum[...] = gpart[pl.ds(pl.multiple_of(core * 64, 64), 64), :] + gpair[...]
     slot = lax.rem(z, 8)
     final = lax.rem(z + 4, 8)
@@ -211,7 +214,7 @@
 
     own.wait()
     for copy in a2a:
-        copy.wait()
+        copy.wait_recv()
     def put(p, cols, value):
         hi, lo = split(value)
         xs[p, pl.ds(0, COLS), cols] = hi
@@ -248,7 +251,7 @@
     w_p = [remote(w2.at[(core, *half(h))], wpair.at[half(h)], wp_s.at[h], wp_r.at[h], partner) for h in halves]
     inner(part)
     for copy in g_rs:
-        copy.wait()
+        copy.wait_recv()
     total = gsum[pl.ds(pl.multiple_of(slot * GCHUNK, GCHUNK), GCHUNK), :]
     for n in range(len(NEAR)):
         total = total + grs[n]
@@ -258,7 +261,7 @@
 
     w_rs = []
     for h in halves:
-        w_p[h].wait()
+        w_p[h].wait_recv()
         wsum[half(h)] = w2[(part, *half(h))] + wpair[half(h)]
         w_rs.append([
             remote(wsum.at[spot(h, slot_of(d))], wrs.at[h, n], wrs_s.at[h, n], wrs_r.at[h, n], along_z(d))
@@ -278,7 +281,7 @@
 
     def exchange(h):
         for copy in w_rs[h]:
-            copy.wait()
+            copy.wait_recv()
         total = wsum[spot(h, slot)]
         for n in range(len(NEAR)):
             total = total + wrs[h, n]
@@ -291,7 +294,7 @@
     for h in halves[: PARTS // 2]:
         exchange(h)
     for copy in g_x:
-        copy.wait()
+        copy.wait_recv()
     ghalf = gi * 128 + core * 64
     gspot = (pl.ds(pl.multiple_of(ghalf + final * GCHUNK, GCHUNK), GCHUNK), bj)
     gfull[gspot] = (gx[0] + gx[1]) + (gx[2] + gx[3])
@@ -301,14 +304,14 @@
     for h in halves[PARTS // 2 :]:
         exchange(h)
     for copy in g_ag:
-        copy.wait()
+        copy.wait_recv()
     gown = gfull.at[pl.ds(pl.multiple_of(ghalf, 64), 64), bj]
     g_xy = [remote(gown, gown, gxy_s.at[n], gxy_r.at[n], in_plane(a, b)) for n, (a, b) in enumerate(XY)]
 
     w_ag = []
     for h in halves:
         for copy in w_x[h]:
-            copy.wait()
+            copy.wait_recv()
         at = wfull.at[(part, *spot(h, final))]
         wfull[(part, *spot(h, final))] = (wx[h, 0] + wx[h, 1]) + (wx[h, 2] + wx[h, 3])
         w_ag.append([
@@ -318,14 +321,14 @@
 
     def hand_over(h):
         for copy in w_ag[h]:
-            copy.wait()
+            copy.wait_recv()
         at = wfull.at[(part, *half(h))]
         w_c.append(remote(at, at, wc_s.at[h], wc_r.at[h], partner))
 
     for h in halves[:-1]:
         hand_over(h)
     for copy in g_xy:
-        copy.wait()
+        copy.wait_recv()
     g_c = []
     for i in range(4):
         strip = gfull.at[pl.ds(pl.multiple_of(i * 128 + core * 64, 64), 64), :]
@@ -342,7 +345,7 @@
         cur[...] = update(0, cur[...], hi, lo)
 
     for copy in g_c:
-        copy.wait()
+        copy.wait_recv()
     gh[...], gl[...] = split(gfull[...])
 
     @pl.when(core == 1)
@@ -350,7 +353,7 @@
         apply_a()
 
     for copy in w_c:
-        copy.wait()
+        copy.wait_recv()
 
     @pl.when(core == 0)
     def _():
@@ -366,6 +369,9 @@
         xh, xl = split(jnp.where(c == 1, cur[tail, :], after_b))
         moved = three(mm, ph[...], pl_[...], xh, xl)
         out_ref[tail, :] = jnp.where(c == 0, after_b, after_b - moved)
+
+    for copy in sent:
+        copy.wait_send()
 
 
 def per_device(eigvecs, reflectors, t_factor, offsets):

time: 72.3 us -> 70.2 us (0.971)
  Pallas kernels: 70.7 us -> 68.6 us
    pallas_call x1, Pallas kernels: 70.7 us -> 68.6 us  [per_device(): pl.pallas_call(kernel, out_shape=jax.ShapeDtypeStruct((ROWS, COLS), F32),...]
where the time goes in v8:
time: 70.2 us; the launch traced here: 70 us
  Pallas kernels  68.6 us (98%)
  local copies, waits for them, and re-layouts  1.4 us (2%)
    pallas_call x1, Pallas kernels, per_device(): pl.pallas_call(kernel, out_shape=jax.ShapeDtypeStruct((ROWS, COLS), F32),...  68.6 us

profile of v8, /device:TPU:1, one launch (start us, length us, event | category | flops | bytes accessed | tf_op | source)
XLA Modules:
  0.0 70.0 jit_solution(4341714641475691893)
XLA Ops:
  0.0 0.0 copy-start
  0.0 0.7 copy-done
  0.7 68.6 %panels.1 = f32[768,128]{1,0:T(8,128)S(1)} custom-call(s32[3]{0:T(128)S(1)} %copy-done, f32[48,2048]{1,0:T(8,128)} %x_hbm.1, f32[3,768,512]{2,1,0:T(8,128)} %v_hbm.1, f32[3,512,512]{2,1,0:T(8,128)} %t_hbm.1), custom_call_target="tpu_custom_call" | custom-call | flops 3000000000 | bytes 9000000 | tf_op jit(solution)/shard_map/panels/pallas_call | solution.py:381
  69.3 0.7 %copy.6 = f32[768,128]{1,0:T(8,128)} copy(f32[768,128]{1,0:T(8,128)S(1)} %panels.1) | data formatting | bytes 786432
Async XLA Ops:
  0.0 0.7 copy-start

commit v9 on v8

--- a/solution.py
+++ b/solution.py
@@ -16,7 +16,10 @@
 LAST = 64 * ROWS - PANEL
 NEAR = (4, 3, -3, 2, -2, 1, -1)
 FAR = (12, -12, 4, -4)
-XY = tuple((a, b) for a in range(NX) for b in range(NY) if (a, b) != (0, 0))
+XY = sorted(
+    ((a, b) for a in range(NX) for b in range(NY) if (a, b) != (0, 0)),
+    key=lambda p: (-min(p[0], NX - p[0]) - min(p[1], NY - p[1]), p),
+)
 HALF, LANES = COLS // 2, 512
 PARTS = 2 * PANEL // LANES
 CHUNK = HALF // 8

time: 70.2 us -> 69.6 us (level)
  no operation moved by 1% of the time
where the time goes in v9:
time: 69.6 us; the launch traced here: 69.4 us
  Pallas kernels  68 us (98%)
  local copies, waits for them, and re-layouts  1.4 us (2%)
    pallas_call x1, Pallas kernels, per_device(): pl.pallas_call(kernel, out_shape=jax.ShapeDtypeStruct((ROWS, COLS), F32),...  68 us
    unnamed x3, local copies, waits for them, and re-layouts  1.4 us

profile of v9, /device:TPU:1, one launch (start us, length us, event | category | flops | bytes accessed | tf_op | source)
XLA Modules:
  0.0 69.4 jit_solution(14878583006123692755)
XLA Ops:
  0.0 0.0 copy-start
  0.0 0.7 copy-done
  0.7 68.0 %panels.1 = f32[768,128]{1,0:T(8,128)S(1)} custom-call(s32[3]{0:T(128)S(1)} %copy-done, f32[48,2048]{1,0:T(8,128)} %x_hbm.1, f32[3,768,512]{2,1,0:T(8,128)} %v_hbm.1, f32[3,512,512]{2,1,0:T(8,128)} %t_hbm.1), custom_call_target="tpu_custom_call" | custom-call | flops 3000000000 | bytes 9000000 | tf_op jit(solution)/shard_map/panels/pallas_call | solution.py:384
  68.7 0.7 %copy.6 = f32[768,128]{1,0:T(8,128)} copy(f32[768,128]{1,0:T(8,128)S(1)} %panels.1) | data formatting | bytes 786432
Async XLA Ops:
  0.0 0.7 copy-start
